TPU v7x, 32 devices: a whole 2x2x4 slice. The times are simulated.
32 devices in a mesh: dp: 4 (over x, core), seq: 8 (over z, y).
Axes of the slice: x: 2, y: 2, z: 4, core: 2. Of those that a mesh axis runs over, the one named last changes fastest.
Arguments:
- inputs: bfloat16 [4, 2048, 1024], P('dp', 'seq'), may hold values from -6 to 6
- cotangent: bfloat16 [4, 2048, 1024], P('dp', 'seq'), may hold values from -6 to 6
- w_qkv: bfloat16 [1024, 3072], P(('dp', 'seq')), may hold values from -0.1875 to 0.1875
- bias_q: bfloat16 [1024], P(('dp', 'seq')), may hold values from -4 to 4
- bias_v: bfloat16 [1024], P(('dp', 'seq')), may hold values from -0.4375 to 0.4375
- w_out: bfloat16 [1024, 1024], P(('dp', 'seq')), may hold values from -2 to 2
- bias_out: bfloat16 [1024], P(('dp', 'seq')), may hold values from -4 to 4
- gain_one: bfloat16 [1024], P(('dp', 'seq')), may hold values from 0.099609375 to 1.8984375
- shift_one: bfloat16 [1024], P(('dp', 'seq')), may hold values from -4 to 4
- w_in: bfloat16 [1024, 4096], P(('dp', 'seq')), may hold values from -0.1875 to 0.1875
- bias_in: bfloat16 [4096], P(('dp', 'seq')), may hold values from -4 to 4
- w_back: bfloat16 [4096, 1024], P(('dp', 'seq')), may hold values from -0.09375 to 0.09375
- bias_back: bfloat16 [1024], P(('dp', 'seq')), may hold values from -4 to 4
- gain_two: bfloat16 [1024], P(('dp', 'seq')), may hold values from 0.099609375 to 1.8984375
- shift_two: bfloat16 [1024], P(('dp', 'seq')), may hold values from -4 to 4
Outputs:
- mixed: bfloat16 [4, 2048, 1024], P('dp', 'seq')
- input_grad: float32 [4, 2048, 1024], P('dp', 'seq')
- grad_w_qkv: float32 [1024, 3072], P(('dp', 'seq'))
- grad_bias_q: float32 [1024], P(('dp', 'seq'))
- grad_bias_v: float32 [1024], P(('dp', 'seq'))
- grad_w_out: float32 [1024, 1024], P(('dp', 'seq'))
- grad_bias_out: float32 [1024], P(('dp', 'seq'))
- grad_gain_one: float32 [1024], P(('dp', 'seq'))
- grad_shift_one: float32 [1024], P(('dp', 'seq'))
- grad_w_in: float32 [1024, 4096], P(('dp', 'seq'))
- grad_bias_in: float32 [4096], P(('dp', 'seq'))
- grad_w_back: float32 [4096, 1024], P(('dp', 'seq'))
- grad_bias_back: float32 [1024], P(('dp', 'seq'))
- grad_gain_two: float32 [1024], P(('dp', 'seq'))
- grad_shift_two: float32 [1024], P(('dp', 'seq'))
All inputs are finite; a program needn't handle non-finite values.
Results may differ from a plain program's by a relative error of at most 0.024.
Values may be sent and summed in bfloat16 or wider, within the bound.
A program may use at most 192 MiB of HBM per device.

v0:
```python
from functools import partial

import jax
import jax.numpy as jnp
from jax import lax
from jax.sharding import PartitionSpec as P

D = 1024
H = 16
HD = 64


EPSILON = 1e-06
ROOT_HALF = 0.7071067811865476
INV_ROOT_TAU = 0.3989422804014327


def layer_stats(values):
    row_mean = jnp.mean(values, axis=-1, keepdims=True)
    centered = values - row_mean
    inv_std = lax.rsqrt(jnp.mean(centered * centered, axis=-1, keepdims=True) + EPSILON)
    return (centered * inv_std, inv_std)


def norm_back(grad_rows, normed, inv_std, gain_row):
    scaled = grad_rows * gain_row
    return inv_std * (
        scaled
        - jnp.mean(scaled, axis=-1, keepdims=True)
        - normed * jnp.mean(scaled * normed, axis=-1, keepdims=True)
    )


def gelu_exact(values):
    return 0.5 * values * (1.0 + lax.erf(values * ROOT_HALF))


def gelu_slope(values):
    return (
        0.5 * (1.0 + lax.erf(values * ROOT_HALF))
        + values * jnp.exp(-0.5 * values * values) * INV_ROOT_TAU
    )


def dense(left, right):
    return jnp.dot(left, right, preferred_element_type=jnp.float32)


def dense_left_t(left, right):
    return lax.dot_general(
        left, right, (((0,), (0,)), ((), ())), preferred_element_type=jnp.float32
    )


def dense_right_t(left, right):
    return lax.dot_general(
        left, right, (((1,), (1,)), ((), ())), preferred_element_type=jnp.float32
    )


def attend_piece(running, pieces, offset, queries, scale):
    acc_rows, row_best, row_total = running
    rows_here = queries.shape[0]
    key_rows = pieces[0].reshape(-1, H, HD)
    value_rows = pieces[1].reshape(-1, H, HD)
    scores = (
        jnp.einsum("qhd,khd->hqk", queries, key_rows, preferred_element_type=jnp.float32) * scale
    )
    new_best = jnp.maximum(row_best, jnp.max(scores, axis=-1))
    rescale = jnp.exp(row_best - new_best)
    shifted = jnp.exp(scores - new_best[:, :, None])
    row_total = row_total * rescale + jnp.sum(shifted, axis=-1)
    partial_out = jnp.einsum(
        "hqk,khd->qhd", shifted.astype(jnp.bfloat16), value_rows, preferred_element_type=jnp.float32
    )
    acc_rows = acc_rows.reshape(rows_here, H, HD) * jnp.transpose(rescale)[:, :, None] + partial_out
    return (acc_rows.reshape(rows_here, H * HD), new_best, row_total)


def attend_back(running, pieces, offset, queries, grad_heads, log_total, delta, scale):
    grad_query, grad_key, grad_value = running
    rows_here = queries.shape[0]
    piece_rows = pieces[0].shape[0]
    key_rows = pieces[0].reshape(piece_rows, H, HD)
    value_rows = pieces[1].reshape(piece_rows, H, HD)
    scores = (
        jnp.einsum("qhd,khd->hqk", queries, key_rows, preferred_element_type=jnp.float32) * scale
    )
    soft_weights = jnp.exp(scores - log_total[:, :, None])
    value_piece = jnp.einsum(
        "hqk,qhd->khd",
        soft_weights.astype(jnp.bfloat16),
        grad_heads,
        preferred_element_type=jnp.float32,
    )
    grad_soft = jnp.einsum(
        "qhd,khd->hqk", grad_heads, value_rows, preferred_element_type=jnp.float32
    )
    grad_scores = (soft_weights * (grad_soft - delta[:, :, None])).astype(jnp.bfloat16)
    query_part = (
        jnp.einsum("hqk,khd->qhd", grad_scores, key_rows, preferred_element_type=jnp.float32)
        * scale
    )
    grad_query = grad_query + query_part.reshape(rows_here, H * HD)
    key_piece = (
        jnp.einsum("hqk,qhd->khd", grad_scores, queries, preferred_element_type=jnp.float32) * scale
    )
    grad_key = lax.dynamic_update_slice_in_dim(
        grad_key, key_piece.reshape(piece_rows, H * HD), offset, 0
    )
    grad_value = lax.dynamic_update_slice_in_dim(
        grad_value, value_piece.reshape(piece_rows, H * HD), offset, 0
    )
    return (grad_query, grad_key, grad_value)


def local_fold(step, initial, gathered, piece_rows):

    def turn(index_turn, running):
        offset = index_turn * piece_rows
        pieces = (
            lax.dynamic_slice_in_dim(gathered[0], offset, piece_rows, 0),
            lax.dynamic_slice_in_dim(gathered[1], offset, piece_rows, 0),
        )
        return step(running, pieces, offset)

    return lax.fori_loop(0, gathered[0].shape[0] // piece_rows, turn, initial)


def per_device(
    inputs,
    cotangent,
    w_qkv,
    bias_q,
    bias_v,
    w_out,
    bias_out,
    gain_one,
    shift_one,
    w_in,
    bias_in,
    w_back,
    bias_back,
    gain_two,
    shift_two,
):
    full_fwd = (
        lax.all_gather(w_qkv, ("dp", "seq"), axis=0, tiled=True),
        lax.all_gather(bias_q, ("dp", "seq"), axis=0, tiled=True),
        lax.all_gather(bias_v, ("dp", "seq"), axis=0, tiled=True),
        lax.all_gather(w_out, ("dp", "seq"), axis=0, tiled=True),
        lax.all_gather(bias_out, ("dp", "seq"), axis=0, tiled=True),
        lax.all_gather(gain_one, ("dp", "seq"), axis=0, tiled=True),
        lax.all_gather(shift_one, ("dp", "seq"), axis=0, tiled=True),
        lax.all_gather(w_in, ("dp", "seq"), axis=0, tiled=True),
        lax.all_gather(bias_in, ("dp", "seq"), axis=0, tiled=True),
        lax.all_gather(w_back, ("dp", "seq"), axis=0, tiled=True),
        lax.all_gather(bias_back, ("dp", "seq"), axis=0, tiled=True),
        lax.all_gather(gain_two, ("dp", "seq"), axis=0, tiled=True),
        lax.all_gather(shift_two, ("dp", "seq"), axis=0, tiled=True),
    )
    (
        wide_qkv,
        full_bq,
        full_bv,
        wide_out,
        full_bo,
        full_g1,
        full_s1,
        wide_in,
        full_b1,
        wide_back,
        full_b2,
        full_g2,
        full_s2,
    ) = full_fwd
    sequence = inputs[0]
    rows_here = sequence.shape[0]
    length_all = rows_here * lax.axis_size("seq")
    scale = HD ** (-0.5)
    projected = dense(sequence, wide_qkv)
    queries = (projected[:, :D] + full_bq.astype(jnp.float32)).astype(jnp.bfloat16)
    key_rows = projected[:, D : 2 * D].astype(jnp.bfloat16)
    value_rows = (projected[:, 2 * D :] + full_bv.astype(jnp.float32)).astype(jnp.bfloat16)
    query_heads = queries.reshape(rows_here, H, HD)
    start_state = (
        jnp.zeros((rows_here, D), jnp.float32),
        jnp.full((H, rows_here), -1e30, jnp.float32),
        jnp.zeros((H, rows_here), jnp.float32),
    )
    forward_step = partial(attend_piece, queries=query_heads, scale=scale)
    whole_pair = (
        lax.all_gather(key_rows, "seq", axis=0, tiled=True),
        lax.all_gather(value_rows, "seq", axis=0, tiled=True),
    )
    acc_rows, row_best, row_total = local_fold(forward_step, start_state, whole_pair, rows_here)
    attended_full = (
        acc_rows.reshape(rows_here, H, HD) / jnp.transpose(row_total)[:, :, None]
    ).reshape(rows_here, D)
    log_total = row_best + jnp.log(row_total)
    attended = attended_full.astype(jnp.bfloat16)
    hidden = sequence.astype(jnp.float32) + dense(attended, wide_out) + full_bo.astype(jnp.float32)
    normed_one, inv_one = layer_stats(hidden)
    first = normed_one * full_g1.astype(jnp.float32) + full_s1.astype(jnp.float32)
    first_low = first.astype(jnp.bfloat16)
    inner = dense(first_low, wide_in) + full_b1.astype(jnp.float32)
    gated = gelu_exact(inner).astype(jnp.bfloat16)
    result = first + dense(gated, wide_back) + full_b2.astype(jnp.float32)
    normed_two, inv_two = layer_stats(result)
    mixed = (normed_two * full_g2.astype(jnp.float32) + full_s2.astype(jnp.float32)).astype(
        jnp.bfloat16
    )
    full_back = (
        lax.all_gather(w_qkv, ("dp", "seq"), axis=0, tiled=True),
        lax.all_gather(bias_q, ("dp", "seq"), axis=0, tiled=True),
        lax.all_gather(bias_v, ("dp", "seq"), axis=0, tiled=True),
        lax.all_gather(w_out, ("dp", "seq"), axis=0, tiled=True),
        lax.all_gather(bias_out, ("dp", "seq"), axis=0, tiled=True),
        lax.all_gather(gain_one, ("dp", "seq"), axis=0, tiled=True),
        lax.all_gather(shift_one, ("dp", "seq"), axis=0, tiled=True),
        lax.all_gather(w_in, ("dp", "seq"), axis=0, tiled=True),
        lax.all_gather(bias_in, ("dp", "seq"), axis=0, tiled=True),
        lax.all_gather(w_back, ("dp", "seq"), axis=0, tiled=True),
        lax.all_gather(bias_back, ("dp", "seq"), axis=0, tiled=True),
        lax.all_gather(gain_two, ("dp", "seq"), axis=0, tiled=True),
        lax.all_gather(shift_two, ("dp", "seq"), axis=0, tiled=True),
    )
    (
        wide_qkv,
        full_bq,
        full_bv,
        wide_out,
        full_bo,
        full_g1,
        full_s1,
        wide_in,
        full_b1,
        wide_back,
        full_b2,
        full_g2,
        full_s2,
    ) = full_back
    grad_rows = cotangent[0].astype(jnp.float32)
    grad_gain_two = jnp.sum(grad_rows * normed_two, axis=0)
    grad_shift_two = jnp.sum(grad_rows, axis=0)
    grad_result = norm_back(grad_rows, normed_two, inv_two, full_g2.astype(jnp.float32))
    grad_bias_back = jnp.sum(grad_result, axis=0)
    result_low = grad_result.astype(jnp.bfloat16)
    grad_w_back = dense_left_t(gated, result_low)
    grad_inner = (dense_right_t(result_low, wide_back) * gelu_slope(inner)).astype(jnp.bfloat16)
    grad_bias_in = jnp.sum(grad_inner.astype(jnp.float32), axis=0)
    grad_w_in = dense_left_t(first_low, grad_inner)
    grad_first = grad_result + dense_right_t(grad_inner, wide_in)
    grad_gain_one = jnp.sum(grad_first * normed_one, axis=0)
    grad_shift_one = jnp.sum(grad_first, axis=0)
    grad_hidden = norm_back(grad_first, normed_one, inv_one, full_g1.astype(jnp.float32))
    grad_bias_out = jnp.sum(grad_hidden, axis=0)
    hidden_low = grad_hidden.astype(jnp.bfloat16)
    grad_w_out = dense_left_t(attended, hidden_low)
    grad_att = dense_right_t(hidden_low, wide_out).astype(jnp.bfloat16)
    grad_heads = grad_att.reshape(rows_here, H, HD)
    delta = jnp.transpose(
        jnp.sum(grad_heads.astype(jnp.float32) * attended_full.reshape(rows_here, H, HD), axis=-1)
    )
    back_state = (
        jnp.zeros((rows_here, D), jnp.float32),
        jnp.zeros((length_all, D), jnp.float32),
        jnp.zeros((length_all, D), jnp.float32),
    )
    backward_step = partial(
        attend_back,
        queries=query_heads,
        grad_heads=grad_heads,
        log_total=log_total,
        delta=delta,
        scale=scale,
    )
    grad_query, key_buffer, value_buffer = local_fold(
        backward_step, back_state, whole_pair, rows_here
    )
    key_sum, value_sum = (
        lax.psum_scatter(
            key_buffer.astype(jnp.bfloat16), "seq", scatter_dimension=0, tiled=True
        ).astype(jnp.float32),
        lax.psum_scatter(
            value_buffer.astype(jnp.bfloat16), "seq", scatter_dimension=0, tiled=True
        ).astype(jnp.float32),
    )
    grad_q_low = grad_query.astype(jnp.bfloat16)
    grad_v_low = value_sum.astype(jnp.bfloat16)
    grad_proj = jnp.concatenate([grad_q_low, key_sum.astype(jnp.bfloat16), grad_v_low], axis=1)
    grad_w_qkv = dense_left_t(sequence, grad_proj)
    grad_bias_q = jnp.sum(grad_q_low.astype(jnp.float32), axis=0)
    grad_bias_v = jnp.sum(grad_v_low.astype(jnp.float32), axis=0)
    input_grad = grad_hidden + dense_right_t(grad_proj, wide_qkv)
    owned = (
        lax.psum_scatter(grad_w_qkv, ("dp", "seq"), scatter_dimension=0, tiled=True),
        lax.psum_scatter(grad_bias_q, ("dp", "seq"), scatter_dimension=0, tiled=True),
        lax.psum_scatter(grad_bias_v, ("dp", "seq"), scatter_dimension=0, tiled=True),
        lax.psum_scatter(grad_w_out, ("dp", "seq"), scatter_dimension=0, tiled=True),
        lax.psum_scatter(grad_bias_out, ("dp", "seq"), scatter_dimension=0, tiled=True),
        lax.psum_scatter(grad_gain_one, ("dp", "seq"), scatter_dimension=0, tiled=True),
        lax.psum_scatter(grad_shift_one, ("dp", "seq"), scatter_dimension=0, tiled=True),
        lax.psum_scatter(grad_w_in, ("dp", "seq"), scatter_dimension=0, tiled=True),
        lax.psum_scatter(grad_bias_in, ("dp", "seq"), scatter_dimension=0, tiled=True),
        lax.psum_scatter(grad_w_back, ("dp", "seq"), scatter_dimension=0, tiled=True),
        lax.psum_scatter(grad_bias_back, ("dp", "seq"), scatter_dimension=0, tiled=True),
        lax.psum_scatter(grad_gain_two, ("dp", "seq"), scatter_dimension=0, tiled=True),
        lax.psum_scatter(grad_shift_two, ("dp", "seq"), scatter_dimension=0, tiled=True),
    )
    (
        own_qkv,
        own_bq,
        own_bv,
        own_out,
        own_bo,
        own_g1,
        own_s1,
        own_in,
        own_b1,
        own_back,
        own_b2,
        own_g2,
        own_s2,
    ) = owned
    return (
        mixed[None],
        input_grad[None],
        own_qkv,
        own_bq,
        own_bv,
        own_out,
        own_bo,
        own_g1,
        own_s1,
        own_in,
        own_b1,
        own_back,
        own_b2,
        own_g2,
        own_s2,
    )


def solution(mesh):
    return jax.shard_map(
        per_device,
        mesh=mesh,
        in_specs=(
            P("dp", "seq", None),
            P("dp", "seq", None),
            P(("dp", "seq"), None),
            P(("dp", "seq")),
            P(("dp", "seq")),
            P(("dp", "seq"), None),
            P(("dp", "seq")),
            P(("dp", "seq")),
            P(("dp", "seq")),
            P(("dp", "seq"), None),
            P(("dp", "seq")),
            P(("dp", "seq"), None),
            P(("dp", "seq")),
            P(("dp", "seq")),
            P(("dp", "seq")),
        ),
        out_specs=(
            P("dp", "seq", None),
            P("dp", "seq", None),
            P(("dp", "seq"), None),
            P(("dp", "seq")),
            P(("dp", "seq")),
            P(("dp", "seq"), None),
            P(("dp", "seq")),
            P(("dp", "seq")),
            P(("dp", "seq")),
            P(("dp", "seq"), None),
            P(("dp", "seq")),
            P(("dp", "seq"), None),
            P(("dp", "seq")),
            P(("dp", "seq")),
            P(("dp", "seq")),
        ),
        check_vma=False,
    )
```

profile of v0, /device:TPU:0, one launch (start us, length us, event | category | flops | bytes accessed | tf_op | source)
XLA Modules:
  0.0 1802.4 jit_solution(13991497408944559826)
XLA Ops:
  8.0 75.1 %all-gather.8.cloned.1.call-done = bf16[1024,3072]{1,0:T(8,128)(2,1)} async-done(((bf16[32,3072]{1,0:T(8,128)(2,1)}), bf16[1024,3072]{1,0:T(8,128)(2,1)}) %all-gather.8.cloned.1.call-update) | async-done | bytes 6291472 | tf_op jit(solution)/shard_map/all_gather | solution.py:148
  83.2 4.8 fusion.45
  90.8 40.2 %all-reduce.18 = (bf16[1024]{0:T(1024)(128)(2,1)S(1)}, bf16[1024]{0:T(1024)(128)(2,1)S(1)}, bf16[1024]{0:T(1024)(128)(2,1)S(1)}, bf16[1024]{0:T(1024)(128)(2,1)S...) all-reduce(bf16[1024]{0:T(1024)(128)(2,1)S(1)} %dynamic-update-slic, ...), channel_id=1, replica_groups=mesh['dp'=4,'seq'=8] {'dp','seq'}, use_global_device_ids=true, to_apply=%add | all-reduce | flops 8192 | bytes 32768
  134.1 65.9 %all-gather = bf16[32,1,128]{2,1,0:T(2,128)(2,1)S(1)} all-gather(bf16[1,1,128]{2,1,0:T(2,128)(2,1)S(1)} %bitcast.174), channel_id=1, replica_groups=mesh['dp'=4,'seq'=8] {'dp','seq'}, dimensions={0}, use_global_device_ids=true | all-gather | bytes 8448 | tf_op jit(solution)/shard_map/all_gather | solution.py:156
  201.3 6.6 copy.52
  207.9 29.0 %all-gather.12.cloned.1.call-done = bf16[2048,1024]{1,0:T(8,128)(2,1)} async-done(((bf16[256,1024]{1,0:T(8,128)(2,1)}), bf16[2048,1024]{1,0:T(8,128)(2,1)}) %all-gather.12.cloned.1.call-update) | async-done | bytes 4194320 | tf_op jit(solution)/shard_map/all_gather | solution.py:194
  236.9 6.5 copy.53
  243.5 65.8 %while.36 = (s32[]{:T(128)}, f32[256,1024]{0,1:T(8,128)S(1)}, f32[16,256]{1,0:T(8,128)S(1)}, f32[16,256]{1,0:T(8,128)S(1)}, bf16[2048,1024]{0,1:T(8,128)(2,1)}, ...) while((s32[]{:T(128)}, f32[256,1024]{0,1:T(8,128)S(1)}, ...), condition=%wide.region_3.0_spmd.clone, body=%wide.region_0.0_spmd.clone.sunk | while | flops 277372928 | bytes 35389644 | solution.py:127
  244.8 2.7 bitcast_reduce_fusion.2
  247.6 3.3 fusion.113
  253.0 2.7 bitcast_reduce_fusion.2
  255.8 3.3 fusion.113
  264.0 3.3 fusion.113
  269.5 2.7 bitcast_reduce_fusion.2
  272.2 3.3 fusion.113
  277.7 2.7 bitcast_reduce_fusion.2
  280.4 3.3 fusion.113
  285.9 2.7 bitcast_reduce_fusion.2
  288.6 3.4 fusion.113
  294.2 2.7 bitcast_reduce_fusion.2
  296.9 3.3 fusion.113
  305.1 3.4 fusion.113
  312.5 61.2 %all-gather.16.cloned.1.call-done = bf16[1024,4096]{1,0:T(8,128)(2,1)} async-done(((bf16[32,4096]{1,0:T(8,128)(2,1)}), bf16[1024,4096]{1,0:T(8,128)(2,1)}) %all-gather.16.cloned.1.call-update) | async-done | bytes 8388624 | tf_op jit(solution)/shard_map/all_gather | solution.py:155
  373.7 7.8 convolution_add_fusion
  381.5 71.1 %all-gather.18.cloned.1.call-done = bf16[4096,1024]{1,0:T(8,128)(2,1)} async-done(((bf16[128,1024]{1,0:T(8,128)(2,1)}), bf16[4096,1024]{1,0:T(8,128)(2,1)}) %all-gather.18.cloned.1.call-update) | async-done | bytes 8388624 | tf_op jit(solution)/shard_map/all_gather | solution.py:157
  452.6 7.2 fusion.62
  461.9 7.0 convert_reduce_fusion
  479.3 109.3 %while.37 = (s32[]{:T(128)}, f32[256,1024]{0,1:T(8,128)}, bf16[2048,1024]{0,1:T(8,128)(2,1)}, bf16[2048,1024]{0,1:T(8,128)(2,1)}, bf16[2048,1024]{0,1:T(8,128)(2...) while((s32[]{:T(128)}, f32[256,1024]{0,1:T(8,128)}, ...), condition=%wide.region_14.0_spmd.clone, body=%wide.region_13.0_spmd.clone.sunk | while | flops 680787968 | bytes 48808172 | solution.py:127
  487.8 3.0 fusion.127
  501.5 3.0 fusion.127
  515.1 3.0 fusion.127
  528.9 3.0 fusion.127
  542.5 3.0 fusion.127
  556.3 3.0 fusion.127
  570.0 3.0 fusion.127
  583.7 3.0 fusion.127
  593.0 82.9 %reduce-scatter.11.cloned.1.call-done = bf16[256,1024]{0,1:T(8,128)(2,1)} async-done(((bf16[2048,1024]{0,1:T(8,128)(2,1)}), bf16[256,1024]{0,1:T(8,128)(2,1)}) %reduce-scatter.11.cloned.1.call-update) | async-done | bytes 524304 | tf_op jit(solution)/shard_map/reduce_scatter | solution.py:285
  675.8 92.3 %reduce-scatter.9.cloned.1.call-done = bf16[256,1024]{0,1:T(8,128)(2,1)} async-done(((bf16[2048,1024]{0,1:T(8,128)(2,1)}), bf16[256,1024]{0,1:T(8,128)(2,1)}) %reduce-scatter.9.cloned.1.call-update) | async-done | bytes 524304 | tf_op jit(solution)/shard_map/reduce_scatter | solution.py:282
  768.2 7.5 convolution_bitcast_fusion
  775.7 12.7 copy.59
  789.6 9.8 fusion.55
  800.7 10.3 fusion.50
  812.4 43.1 %all-reduce.17 = (f32[1024]{0:T(1024)S(1)}, f32[1024]{0:T(1024)S(1)}, f32[1024]{0:T(1024)S(1)}, f32[1024]{0:T(1024)S(1)}, f32[1024]{0:T(1024)S(1)}, /*index=5*/f...) all-reduce(f32[1024]{0:T(1024)S(1)} %get-tuple-element.535, ...), channel_id=5, replica_groups=mesh['dp'=4,'seq'=8] {'dp','seq'}, use_global_device_ids=true, to_apply=%region_19.0.clone | all-reduce | flops 12288 | bytes 98304
  860.8 5.6 fusion.33
  866.4 48.8 %reduce-scatter.13.cloned.1.call-done = f32[32,1024]{1,0:T(8,128)} async-done(((f32[1024,1024]{1,0:T(8,128)}), f32[32,1024]{1,0:T(8,128)}) %reduce-scatter.13.cloned.1.call-update) | async-done | bytes 131088 | tf_op jit(solution)/shard_map/reduce_scatter | solution.py:300
  915.2 159.6 %reduce-scatter.19.cloned.1.call-done = f32[32,3072]{1,0:T(8,128)} async-done(((f32[1024,3072]{1,0:T(8,128)}), f32[32,3072]{1,0:T(8,128)}) %reduce-scatter.19.cloned.1.call-update) | async-done | bytes 393232
  1074.7 360.2 %reduce-scatter.15.cloned.1.call-done = f32[32,4096]{1,0:T(8,128)} async-done(((f32[1024,4096]{1,0:T(8,128)}), f32[32,4096]{1,0:T(8,128)}) %reduce-scatter.15.cloned.1.call-update) | async-done | bytes 524304 | tf_op jit(solution)/shard_map/reduce_scatter | solution.py:304
  1435.0 360.2 %reduce-scatter.17.cloned.1.call-done = f32[128,1024]{1,0:T(8,128)} async-done(((f32[4096,1024]{1,0:T(8,128)}), f32[128,1024]{1,0:T(8,128)}) %reduce-scatter.17.cloned.1.call-update) | async-done | bytes 524304 | tf_op jit(solution)/shard_map/reduce_scatter | solution.py:306
  (287 shorter events, 143.9 us)
Async XLA Ops:
  7.2 76.0 %all-gather.8.cloned.1.call-start = ((), (), s32[]{:S(2)}) async-start(), calls=%async_computation.6 | async-start | bytes 6488064 | tf_op jit(solution)/shard_map/all_gather | solution.py:148
  7.9 81.0 %copy-start.20 = (bf16[32]{0:T(256)(128)(2,1)S(1)}, bf16[32]{0:T(256)(128)(2,1)}, u32[]{:S(2)}) copy-start(bf16[32]{0:T(256)(128)(2,1)} %param.22) | copy-start | bytes 196
  7.9 81.2 %copy-start.21 = (bf16[32]{0:T(256)(128)(2,1)S(1)}, bf16[32]{0:T(256)(128)(2,1)}, u32[]{:S(2)}) copy-start(bf16[32]{0:T(256)(128)(2,1)} %param.23) | copy-start | bytes 196
  7.9 81.5 %copy-start.22 = (bf16[32]{0:T(256)(128)(2,1)S(1)}, bf16[32]{0:T(256)(128)(2,1)}, u32[]{:S(2)}) copy-start(bf16[32]{0:T(256)(128)(2,1)} %param.25) | copy-start | bytes 196
  7.9 81.7 %copy-start.23 = (bf16[32]{0:T(256)(128)(2,1)S(1)}, bf16[32]{0:T(256)(128)(2,1)}, u32[]{:S(2)}) copy-start(bf16[32]{0:T(256)(128)(2,1)} %param.31) | copy-start | bytes 196
  8.0 81.9 %copy-start.24 = (bf16[32]{0:T(256)(128)(2,1)S(1)}, bf16[32]{0:T(256)(128)(2,1)}, u32[]{:S(2)}) copy-start(bf16[32]{0:T(256)(128)(2,1)} %param.27) | copy-start | bytes 196
  8.0 82.1 %copy-start.25 = (bf16[32]{0:T(256)(128)(2,1)S(1)}, bf16[32]{0:T(256)(128)(2,1)}, u32[]{:S(2)}) copy-start(bf16[32]{0:T(256)(128)(2,1)} %param.26) | copy-start | bytes 196
  8.0 82.4 %copy-start.26 = (bf16[32]{0:T(256)(128)(2,1)S(1)}, bf16[32]{0:T(256)(128)(2,1)}, u32[]{:S(2)}) copy-start(bf16[32]{0:T(256)(128)(2,1)} %param.33) | copy-start | bytes 196
  8.0 82.6 %copy-start.27 = (bf16[32]{0:T(256)(128)(2,1)S(1)}, bf16[32]{0:T(256)(128)(2,1)}, u32[]{:S(2)}) copy-start(bf16[32]{0:T(256)(128)(2,1)} %param.32) | copy-start | bytes 196
  8.0 193.3 %all-gather.10.cloned.1.call-start = ((), (), s32[]{:S(2)}) async-start(), calls=%async_computation.7 | async-start | bytes 4718592 | tf_op jit(solution)/shard_map/all_gather | solution.py:193
  87.9 46.1 %copy-start.19 = (bf16[128]{0:T(256)(128)(2,1)S(1)}, bf16[128]{0:T(256)(128)(2,1)}, u32[]{:S(2)}) copy-start(bf16[128]{0:T(256)(128)(2,1)} %param.29) | copy-start | bytes 772
  88.8 148.1 %all-gather.12.cloned.1.call-start = ((), (), s32[]{:S(2)}) async-start(), calls=%async_computation.8 | async-start | bytes 4718592 | tf_op jit(solution)/shard_map/all_gather | solution.py:194
  132.2 177.3 %all-gather.14.cloned.1.call-start = ((), (), s32[]{:S(2)}) async-start(), calls=%async_computation.9 | async-start | bytes 2162688 | tf_op jit(solution)/shard_map/all_gather | solution.py:151
  132.8 240.9 %all-gather.16.cloned.1.call-start = ((), (), s32[]{:S(2)}) async-start(), calls=%async_computation.10 | async-start | bytes 8650752 | tf_op jit(solution)/shard_map/all_gather | solution.py:155
  133.4 319.2 %all-gather.18.cloned.1.call-start = ((), (), s32[]{:S(2)}) async-start(), calls=%async_computation.11 | async-start | bytes 8650752 | tf_op jit(solution)/shard_map/all_gather | solution.py:157
  134.0 541.9 %reduce-scatter.11.cloned.1.call-start = ((), (), s32[]{:S(2)}) async-start(), calls=%async_computation.13 | async-start | bytes 4718592 | tf_op jit(solution)/shard_map/reduce_scatter | solution.py:285
  247.5 3.4 copy-start.1
  255.8 3.4 copy-start.1
  264.0 3.5 copy-start.1
  272.2 3.4 copy-start.1
  280.4 3.5 copy-start.1
  288.6 3.5 copy-start.1
  296.9 3.4 copy-start.1
  305.1 3.5 copy-start.1
  309.5 64.2 %copy-start.11 = (bf16[256,1024]{0,1:T(8,128)(2,1)}, bf16[256,1024]{0,1:T(8,128)(2,1)S(1)}, u32[]{:S(2)}) copy-start(bf16[256,1024]{0,1:T(8,128)(2,1)S(1)} %fusion.41) | copy-start | bytes 1572868
  312.2 159.6 %copy-start.3 = (f32[256,1024]{1,0:T(8,128)}, f32[256,1024]{1,0:T(8,128)S(1)}, u32[]{:S(2)}) copy-start(f32[256,1024]{1,0:T(8,128)S(1)} %get-tuple-element.547) | copy-start | bytes 3145732
  381.5 78.5 %copy-start.9 = (bf16[1,256,1024]{2,1,0:T(8,128)(2,1)S(1)}, bf16[1,256,1024]{2,1,0:T(8,128)(2,1)}, u32[]{:S(2)}) copy-start(bf16[1,256,1024]{2,1,0:T(8,128)(2,1)} %param.20) | copy-start | bytes 1572868
  460.6 8.4 slice-start
  461.9 7.2 copy-start.13
  461.9 7.1 slice-start.1
  469.0 2.8 copy-start.17
  469.1 4.1 copy-start.7
  481.1 2.7 copy-start
  494.5 2.7 copy-start
  508.2 2.7 copy-start
  521.9 2.7 copy-start
  535.6 2.7 copy-start
  549.4 2.7 copy-start
  563.1 2.7 copy-start
  576.7 2.7 copy-start
  588.6 179.5 %reduce-scatter.9.cloned.1.call-start = ((), (), s32[]{:S(2)}) async-start(), calls=%async_computation.12 | async-start | bytes 4718592 | tf_op jit(solution)/shard_map/reduce_scatter | solution.py:282
  589.4 3.3 copy-start.2
  589.4 325.8 %reduce-scatter.13.cloned.1.call-start = ((), (), s32[]{:S(2)}) async-start(), calls=%async_computation.14 | async-start | bytes 4325376 | tf_op jit(solution)/shard_map/reduce_scatter | solution.py:300
  592.7 175.5 %copy-start.15 = (bf16[1,256,1024]{2,1,0:T(8,128)(2,1)S(1)}, bf16[1,256,1024]{2,1,0:T(8,128)(2,1)}, u32[]{:S(2)}) copy-start(bf16[1,256,1024]{2,1,0:T(8,128)(2,1)} %param.19) | copy-start | bytes 1572868
  592.7 482.1 %reduce-scatter.19.cloned.1.call-start = ((), (), s32[]{:S(2)}) async-start(), calls=%async_computation.17 | async-start | bytes 12976128
  788.4 646.6 %reduce-scatter.15.cloned.1.call-start = ((), (), s32[]{:S(2)}) async-start(), calls=%async_computation.15 | async-start | bytes 17301504 | tf_op jit(solution)/shard_map/reduce_scatter | solution.py:304
  799.5 995.7 %reduce-scatter.17.cloned.1.call-start = ((), (), s32[]{:S(2)}) async-start(), calls=%async_computation.16 | async-start | bytes 17301504 | tf_op jit(solution)/shard_map/reduce_scatter | solution.py:306
  811.0 49.8 %copy-start.18 = (bf16[256,1024]{0,1:T(8,128)(2,1)S(1)}, bf16[256,1024]{0,1:T(8,128)(2,1)}, u32[]{:S(2)}) copy-start(bf16[256,1024]{0,1:T(8,128)(2,1)} %reduce-scatter.9.cloned.1.call-done) | copy-start | bytes 1572868
  (8 other events, 10.4 us)
Sparse Core Ops, SparseCore 0:
  10.9 72.2 all-gather.7
  89.0 73.5 all-gather.9
  165.3 71.5 all-gather.11
  239.8 54.7 all-gather.13
  297.4 76.2 all-gather.15
  376.6 75.9 all-gather.17
  588.8 87.0 reduce-scatter.10
  679.9 88.2 reduce-scatter.8
  771.0 144.0 reduce-scatter.12
  921.6 153.0 reduce-scatter.18
  1077.7 357.1 reduce-scatter.14
  1437.8 357.3 reduce-scatter.16
where the time goes:
time: 1810 us; the launch traced here: 1800 us
  waiting for transfers between devices  1340 us (74%)
  matrix products  176 us (10%)
  blocking collectives  149 us (8%)
  local copies, waits for them, and re-layouts  85.8 us (5%)
  other arithmetic  31.7 us (2%)
    reduce_scatter x1, waiting for transfers between devices, per_device(): lax.psum_scatter(grad_w_in, ('dp', 'seq'), scatter_dimension=0, tiled=True)  360 us
    reduce_scatter x1, waiting for transfers between devices, per_device(): lax.psum_scatter(grad_w_back, ('dp', 'seq'), scatter_dimension=0, tiled=T...  360 us
    unnamed x13, waiting for transfers between devices  163 us
    reduce_scatter x1, waiting for transfers between devices, per_device(): lax.psum_scatter(key_buffer.astype(jnp.bfloat16), 'seq', scatter_dimensio...  92.3 us
    unnamed x2, blocking collectives  83.3 us
    reduce_scatter x1, waiting for transfers between devices, per_device(): lax.psum_scatter(value_buffer.astype(jnp.bfloat16), 'seq', scatter_dimens...  82.9 us
    all_gather x1, waiting for transfers between devices, per_device(): lax.all_gather(w_qkv, ('dp', 'seq'), axis=0, tiled=True)  75.1 us
    all_gather x1, waiting for transfers between devices, per_device(): lax.all_gather(w_back, ('dp', 'seq'), axis=0, tiled=True)  71.1 us
  transfers between devices with their start and end apart: 12, of which 10 were waited for; matrix products, arithmetic and copies ran while one was open for 8% of the time, Pallas kernels for 0%

commit v1 on v0

v1 whole, which is shorter than its diff:
```python
import jax
import jax.numpy as jnp
from jax import lax
from jax.experimental import pallas as pl
from jax.experimental.pallas import tpu as pltpu
from jax.sharding import PartitionSpec as P

D = 1024
H = 16
HD = 64


EPSILON = 1e-06
ROOT_HALF = 0.7071067811865476
INV_ROOT_TAU = 0.3989422804014327
SCALE = HD ** (-0.5)
SCALE_LOG2 = SCALE * 1.4426950408889634
VMEM_LIMIT = 48 * 1024 * 1024
AXES = ("dp", "seq")


def layer_stats(values):
    row_mean = jnp.mean(values, axis=-1, keepdims=True)
    centered = values - row_mean
    inv_std = lax.rsqrt(jnp.mean(centered * centered, axis=-1, keepdims=True) + EPSILON)
    return (centered * inv_std, inv_std)


def norm_back(grad_rows, normed, inv_std, gain_row):
    scaled = grad_rows * gain_row
    return inv_std * (
        scaled
        - jnp.mean(scaled, axis=-1, keepdims=True)
        - normed * jnp.mean(scaled * normed, axis=-1, keepdims=True)
    )


def gelu_exact(values):
    return 0.5 * values * (1.0 + lax.erf(values * ROOT_HALF))


def gelu_slope(values):
    return (
        0.5 * (1.0 + lax.erf(values * ROOT_HALF))
        + values * jnp.exp(-0.5 * values * values) * INV_ROOT_TAU
    )


def dense(left, right):
    return jnp.dot(left, right, preferred_element_type=jnp.float32)


def dense_left_t(left, right):
    return lax.dot_general(
        left, right, (((0,), (0,)), ((), ())), preferred_element_type=jnp.float32
    )


def dense_right_t(left, right):
    return lax.dot_general(
        left, right, (((1,), (1,)), ((), ())), preferred_element_type=jnp.float32
    )


def mm(left, right, dims):
    return lax.dot_general(left, right, (dims, ((), ())), preferred_element_type=jnp.float32)


def head_only(block, head):
    lane = lax.broadcasted_iota(jnp.int32, block.shape, 1)
    inside = (lane >= head * HD) & (lane < (head + 1) * HD)
    return jnp.where(inside, block, jnp.zeros_like(block))


def attend_forward_body(q_ref, k_ref, v_ref, low_ref, full_ref, lse_ref, vt_ref):
    groups, _, rows, width = k_ref.shape
    length = groups * rows

    @pl.when(pl.program_id(0) == 0)
    def _():
        vt_ref[...] = v_ref[...].reshape(length, width).T

    keys = k_ref[...].reshape(length, width)
    queries = q_ref[0, 0]
    outs = []
    for head in range(width // HD):
        scores = mm(keys, head_only(queries, head), ((1,), (1,)))
        top = jnp.max(scores, axis=0, keepdims=True) * SCALE_LOG2
        weights = jnp.exp2(scores * SCALE_LOG2 - top)
        total = jnp.sum(weights, axis=0, keepdims=True)
        out_t = mm(vt_ref[head * HD : (head + 1) * HD, :], weights.astype(jnp.bfloat16), ((1,), (0,)))
        outs.append(out_t / total)
        lse_ref[0, head : head + 1, :] = top + jnp.log2(total)
    out = jnp.concatenate(outs, axis=0).T
    full_ref[0] = out
    low_ref[0] = out.astype(jnp.bfloat16)


def attend_forward(packed):
    groups, _, rows, width = packed.shape
    heads = width // HD
    whole = lambda which: pl.BlockSpec((groups, 1, rows, width), lambda i: (0, which, 0, 0))
    own = pl.BlockSpec((1, rows, width), lambda i: (i, 0, 0))
    length = groups * rows
    return pl.pallas_call(
        attend_forward_body,
        grid=(groups,),
        in_specs=[pl.BlockSpec((1, 1, rows, width), lambda i: (i, 0, 0, 0)), whole(1), whole(2)],
        out_specs=[own, own, pl.BlockSpec((1, heads, rows), lambda i: (i, 0, 0))],
        out_shape=[
            jax.ShapeDtypeStruct((groups, rows, width), jnp.bfloat16),
            jax.ShapeDtypeStruct((groups, rows, width), jnp.float32),
            jax.ShapeDtypeStruct((groups, heads, rows), jnp.float32),
        ],
        scratch_shapes=[pltpu.VMEM((width, length), jnp.bfloat16)],
        compiler_params=pltpu.CompilerParams(vmem_limit_bytes=VMEM_LIMIT),
        cost_estimate=pl.CostEstimate(
            flops=16 * length * length * width,
            bytes_accessed=10 * length * width,
            transcendentals=heads * length * length,
        ),
        name="attend_forward",
    )(packed, packed, packed)


def attend_backward_body(
    q_ref, k_ref, v_ref, grad_ref, full_ref, lse_ref, out_ref, kt_ref, dk_ref, dv_ref
):
    groups, _, rows, width = k_ref.shape
    length = groups * rows
    heads = width // HD
    step = pl.program_id(0)

    @pl.when(step == 0)
    def _():
        kt_ref[...] = k_ref[...].reshape(length, width).T
        dk_ref[...] = jnp.zeros_like(dk_ref)
        dv_ref[...] = jnp.zeros_like(dv_ref)

    queries = q_ref[0, 0]
    grads = grad_ref[0]
    spread = (grads.astype(jnp.float32) * full_ref[0]).T
    q_heads = [head_only(queries, head) for head in range(heads)]
    g_heads = [head_only(grads, head) for head in range(heads)]
    deltas = [
        jnp.sum(spread[head * HD : (head + 1) * HD], axis=0, keepdims=True)
        for head in range(heads)
    ]
    dq = [jnp.zeros((HD, rows), jnp.float32) for _ in range(heads)]
    per = min(2, groups)
    piece = per * rows
    for part in range(groups // per):
        keys = k_ref[part * per : (part + 1) * per].reshape(piece, width)
        values = v_ref[part * per : (part + 1) * per].reshape(piece, width)
        span = slice(part * piece, (part + 1) * piece)
        dk_part = dk_ref[span, :]
        dv_part = dv_ref[span, :]
        for head in range(heads):
            scores = mm(keys, q_heads[head], ((1,), (1,)))
            weights = jnp.exp2(scores * SCALE_LOG2 - lse_ref[0, head : head + 1, :])
            d_soft = mm(values, g_heads[head], ((1,), (1,)))
            d_scores = (weights * (d_soft - deltas[head])).astype(jnp.bfloat16)
            dv_part += mm(weights.astype(jnp.bfloat16), g_heads[head], ((1,), (0,)))
            dk_part += mm(d_scores, q_heads[head], ((1,), (0,)))
            dq[head] += mm(kt_ref[head * HD : (head + 1) * HD, span], d_scores, ((1,), (0,)))
        dk_ref[span, :] = dk_part
        dv_ref[span, :] = dv_part
    dq_all = jnp.concatenate(dq, axis=0) if heads > 1 else dq[0]
    out_ref[step, 0] = (dq_all * SCALE).T.astype(jnp.bfloat16)

    @pl.when(step == groups - 1)
    def _():
        out_ref[:, 1] = (dk_ref[...] * SCALE).astype(jnp.bfloat16).reshape(groups, rows, width)
        out_ref[:, 2] = dv_ref[...].astype(jnp.bfloat16).reshape(groups, rows, width)


def attend_backward(packed, grads, full, lse):
    groups, _, rows, width = packed.shape
    heads = width // HD
    length = groups * rows
    whole = lambda which: pl.BlockSpec((groups, 1, rows, width), lambda i: (0, which, 0, 0))
    own = pl.BlockSpec((1, rows, width), lambda i: (i, 0, 0))
    return pl.pallas_call(
        attend_backward_body,
        grid=(groups,),
        in_specs=[
            pl.BlockSpec((1, 1, rows, width), lambda i: (i, 0, 0, 0)),
            whole(1),
            whole(2),
            own,
            own,
            pl.BlockSpec((1, heads, rows), lambda i: (i, 0, 0)),
        ],
        out_specs=pl.BlockSpec((groups, 3, rows, width), lambda i: (0, 0, 0, 0)),
        out_shape=jax.ShapeDtypeStruct((groups, 3, rows, width), jnp.bfloat16),
        scratch_shapes=[
            pltpu.VMEM((width, length), jnp.bfloat16),
            pltpu.VMEM((length, width), jnp.float32),
            pltpu.VMEM((length, width), jnp.float32),
        ],
        compiler_params=pltpu.CompilerParams(vmem_limit_bytes=VMEM_LIMIT),
        cost_estimate=pl.CostEstimate(
            flops=40 * length * length * width,
            bytes_accessed=20 * length * width,
            transcendentals=heads * length * length,
        ),
        name="attend_backward",
    )(packed, packed, packed, grads, full, lse)


def swap(blocks):
    return lax.all_to_all(blocks, "seq", 0, 0, tiled=True)


def gather(shard):
    return lax.all_gather(shard, AXES, axis=0, tiled=True)


def scatter(whole):
    return lax.psum_scatter(whole, AXES, scatter_dimension=0, tiled=True)


def per_device(
    inputs,
    cotangent,
    w_qkv,
    bias_q,
    bias_v,
    w_out,
    bias_out,
    gain_one,
    shift_one,
    w_in,
    bias_in,
    w_back,
    bias_back,
    gain_two,
    shift_two,
):
    groups = lax.axis_size("seq")
    devices = lax.axis_size("dp") * groups
    vectors = (bias_q, bias_v, bias_out, gain_one, shift_one, bias_in, bias_back, gain_two, shift_two)
    wide_qkv = gather(w_qkv)
    rows_of = lax.all_gather(jnp.concatenate(vectors), AXES, axis=0, tiled=False)
    wide_out = gather(w_out)
    wide_in = gather(w_in)
    wide_back = gather(w_back)
    full = []
    place = 0
    for vector in vectors:
        part = rows_of[:, place : place + vector.shape[0]]
        full.append(part.reshape(1, -1).astype(jnp.float32))
        place += vector.shape[0]
    full_bq, full_bv, full_bo, full_g1, full_s1, full_b1, full_b2, full_g2, full_s2 = full

    sequence = inputs[0]
    rows_here = sequence.shape[0]
    width = D // groups
    bias_qkv = jnp.concatenate([full_bq, jnp.zeros_like(full_bq), full_bv], axis=1)
    projected = (dense(sequence, wide_qkv) + bias_qkv).astype(jnp.bfloat16)
    packed = swap(jnp.transpose(projected.reshape(rows_here, 3, groups, width), (2, 1, 0, 3)))
    att_low, att_full, lse = attend_forward(packed)
    attended = jnp.transpose(swap(att_low), (1, 0, 2)).reshape(rows_here, D)

    hidden = sequence.astype(jnp.float32) + dense(attended, wide_out) + full_bo
    normed_one, inv_one = layer_stats(hidden)
    first = normed_one * full_g1 + full_s1
    first_low = first.astype(jnp.bfloat16)
    inner = dense(first_low, wide_in) + full_b1
    gated = gelu_exact(inner).astype(jnp.bfloat16)
    result = first + dense(gated, wide_back) + full_b2
    normed_two, inv_two = layer_stats(result)
    mixed = (normed_two * full_g2 + full_s2).astype(jnp.bfloat16)

    grad_rows = cotangent[0].astype(jnp.float32)
    grad_gain_two = jnp.sum(grad_rows * normed_two, axis=0)
    grad_shift_two = jnp.sum(grad_rows, axis=0)
    grad_result = norm_back(grad_rows, normed_two, inv_two, full_g2)
    grad_bias_back = jnp.sum(grad_result, axis=0)
    result_low = grad_result.astype(jnp.bfloat16)
    own_back = scatter(dense_left_t(gated, result_low).astype(jnp.bfloat16))
    grad_inner = (dense_right_t(result_low, wide_back) * gelu_slope(inner)).astype(jnp.bfloat16)
    grad_bias_in = jnp.sum(grad_inner.astype(jnp.float32), axis=0)
    own_in = scatter(dense_left_t(first_low, grad_inner).astype(jnp.bfloat16))
    grad_first = grad_result + dense_right_t(grad_inner, wide_in)
    grad_gain_one = jnp.sum(grad_first * normed_one, axis=0)
    grad_shift_one = jnp.sum(grad_first, axis=0)
    grad_hidden = norm_back(grad_first, normed_one, inv_one, full_g1)
    grad_bias_out = jnp.sum(grad_hidden, axis=0)
    hidden_low = grad_hidden.astype(jnp.bfloat16)
    own_out = scatter(dense_left_t(attended, hidden_low).astype(jnp.bfloat16))
    grad_att = dense_right_t(hidden_low, wide_out).astype(jnp.bfloat16)
    grad_heads = swap(jnp.transpose(grad_att.reshape(rows_here, groups, width), (1, 0, 2)))
    grad_packed = swap(attend_backward(packed, grad_heads, att_full, lse))
    grad_proj = jnp.transpose(grad_packed, (2, 1, 0, 3)).reshape(rows_here, 3 * D)
    own_qkv = scatter(dense_left_t(sequence, grad_proj).astype(jnp.bfloat16))
    grad_bias_q = jnp.sum(grad_proj[:, :D].astype(jnp.float32), axis=0)
    grad_bias_v = jnp.sum(grad_proj[:, 2 * D :].astype(jnp.float32), axis=0)
    input_grad = grad_hidden + dense_right_t(grad_proj, wide_qkv)

    sums = (
        grad_bias_q,
        grad_bias_v,
        grad_bias_out,
        grad_gain_one,
        grad_shift_one,
        grad_bias_in,
        grad_bias_back,
        grad_gain_two,
        grad_shift_two,
    )
    owned = lax.psum_scatter(
        jnp.concatenate([item.reshape(devices, -1) for item in sums], axis=1),
        AXES,
        scatter_dimension=0,
        tiled=False,
    )
    small = []
    place = 0
    for vector in vectors:
        small.append(owned[place : place + vector.shape[0]])
        place += vector.shape[0]
    own_bq, own_bv, own_bo, own_g1, own_s1, own_b1, own_b2, own_g2, own_s2 = small
    return (
        mixed[None],
        input_grad[None],
        own_qkv.astype(jnp.float32),
        own_bq,
        own_bv,
        own_out.astype(jnp.float32),
        own_bo,
        own_g1,
        own_s1,
        own_in.astype(jnp.float32),
        own_b1,
        own_back.astype(jnp.float32),
        own_b2,
        own_g2,
        own_s2,
    )


def solution(mesh):
    return jax.shard_map(
        per_device,
        mesh=mesh,
        in_specs=(
            P("dp", "seq", None),
            P("dp", "seq", None),
            P(("dp", "seq"), None),
            P(("dp", "seq")),
            P(("dp", "seq")),
            P(("dp", "seq"), None),
            P(("dp", "seq")),
            P(("dp", "seq")),
            P(("dp", "seq")),
            P(("dp", "seq"), None),
            P(("dp", "seq")),
            P(("dp", "seq"), None),
            P(("dp", "seq")),
            P(("dp", "seq")),
            P(("dp", "seq")),
        ),
        out_specs=(
            P("dp", "seq", None),
            P("dp", "seq", None),
            P(("dp", "seq"), None),
            P(("dp", "seq")),
            P(("dp", "seq")),
            P(("dp", "seq"), None),
            P(("dp", "seq")),
            P(("dp", "seq")),
            P(("dp", "seq")),
            P(("dp", "seq"), None),
            P(("dp", "seq")),
            P(("dp", "seq"), None),
            P(("dp", "seq")),
            P(("dp", "seq")),
            P(("dp", "seq")),
        ),
        check_vma=False,
    )
```

time: 1810 us -> 979 us (0.54)
  waiting for transfers between devices: 1340 us -> 605 us
  matrix products: 176 us -> 61 us
  local copies, waits for them, and re-layouts: 85.8 us -> 32.3 us
  blocking collectives: 149 us -> 202 us
  Pallas kernels: 0 us -> 45.9 us
  other arithmetic: 31.7 us -> 8.37 us
    reduce_scatter x5 -> x3, waiting for transfers between devices: 944 us -> 368 us  [scatter(): return lax.psum_scatter(whole, AXES, scatter_dimension=0, tiled=True)]
    all_gather x6 -> x4, waiting for transfers between devices: 237 us -> 115 us  [gather(): return lax.all_gather(shard, AXES, axis=0, tiled=True)]
    dot_general x56 -> x0, matrix products: 107 us -> none  [the longest x8 26.7 us: attend_piece(): jnp.einsum('hqk,khd->qhd', shifted.astype(jnp.bfloat16), value_rows, pref...]
    all_to_all x0 -> x2, blocking collectives: none -> 91.3 us  [swap(): return lax.all_to_all(blocks, 'seq', 0, 0, tiled=True)]
    unnamed x13 -> x9, waiting for transfers between devices: 163 us -> 95.6 us
    pallas_call x0 -> x2, Pallas kernels: none -> 45.9 us  [the longest x1 23.8 us: attend_backward(): pl.pallas_call(attend_backward_body, grid=(groups,), in_specs=[pl.BlockSp...]
    unnamed x2 -> x1, blocking collectives: 83.3 us -> 39.7 us
    dynamic_slice x24 -> x0, local copies, waits for them, and re-layouts: 30.9 us -> none  [the longest x16 22.3 us: turn(): lax.dynamic_slice_in_dim(gathered[1], offset, piece_rows, 0)]
  transfers between devices with their start and end apart: 12 -> 10, of which waited for: 10 -> 7; matrix products, arithmetic and copies ran while one was open for 8% -> 7% of each run, Pallas kernels for 0% -> 5%
where the time goes in v1:
time: 979 us; the launch traced here: 977 us
  waiting for transfers between devices  605 us (62%)
  blocking collectives  202 us (21%)
  matrix products  61 us (6%)
  Pallas kernels  45.9 us (5%)
  local copies, waits for them, and re-layouts  32.3 us (3%)
  between operations  14.5 us (1%)
    reduce_scatter x3, waiting for transfers between devices, scatter(): return lax.psum_scatter(whole, AXES, scatter_dimension=0, tiled=True)  368 us
    all_gather x4, waiting for transfers between devices, gather(): return lax.all_gather(shard, AXES, axis=0, tiled=True)  115 us
    unnamed x9, waiting for transfers between devices  95.6 us
    all_to_all x2, blocking collectives, swap(): return lax.all_to_all(blocks, 'seq', 0, 0, tiled=True)  91.3 us
    all_gather x1, blocking collectives, per_device(): lax.all_gather(jnp.concatenate(vectors), AXES, axis=0, tiled=False)  70.8 us
    unnamed x1, blocking collectives  39.7 us
    all_to_all x2, waiting for transfers between devices, swap(): return lax.all_to_all(blocks, 'seq', 0, 0, tiled=True)  26.5 us
    pallas_call x1, Pallas kernels, attend_backward(): pl.pallas_call(attend_backward_body, grid=(groups,), in_specs=[pl.BlockSp...  23.8 us
  transfers between devices with their start and end apart: 10, of which 7 were waited for; matrix products, arithmetic and copies ran while one was open for 7% of the time, Pallas kernels for 5%

profile of v1, /device:TPU:0, one launch (start us, length us, event | category | flops | bytes accessed | tf_op | source)
XLA Modules:
  0.0 977.4 jit_solution(9735914521203503198)
XLA Ops:
  8.0 0.7 all-gather.9.cloned.1.call-update
  10.0 6.1 concatenate.9
  16.1 70.8 %all-gather.1 = bf16[32,1,384]{2,1,0:T(2,128)(2,1)S(1)} all-gather(bf16[1,1,384]{2,1,0:T(2,128)(2,1)S(1)} %reshape.242), channel_id=2, replica_groups=mesh['dp'=4,'seq'=8] {'dp','seq'}, dimensions={0}, use_global_device_ids=true | all-gather | bytes 25344 | tf_op jit(solution)/shard_map/all_gather | solution.py:244
  87.2 4.8 fusion.5
  92.0 0.7 copy.38
  92.7 0.9 copy.39
  93.6 44.0 %all_to_all.20.q_ref.k_ref.v_ref = bf16[8,3,256,128]{3,2,1,0:T(8,128)(2,1)S(1)} all-to-all(bf16[8,3,256,128]{3,2,1,0:T(8,128)(2,1)S(1)} %bitcast.91), channel_id=1, replica_groups=mesh['dp'=4,'seq'=8] {'seq'}, dimensions={0} | all-to-all | bytes 3145728 | tf_op jit(solution)/shard_map/all_to_all | solution.py:212
  137.6 22.2 %attend_forward.1 = (bf16[8,256,128]{2,1,0:T(8,128)(2,1)}, f32[8,256,128]{2,1,0:T(8,128)S(1)}, f32[8,2,256]{2,1,0:T(2,128)S(1)}) custom-call(bf16[8,3,256,128]{3,2,1,0:T(8,128)(2,1)S(1)} %all_to_all.20.q_ref.k_ref.v_ref, bf16[8,3,256,128]{3,2,1,0:T(8,128)(2,1)S(1)} %all_to_all.20.q_ref.k_ref.v_ref, bf16[8,3,256,128]{3,2,1,0:T(8,128)(2,1)S(1)} %all_to_all.20.q_ref.k_ref.v_ref), custom_call_target="tpu_custom_call" | custom-call | flops 8589934592 | bytes 2621440 | tf_op jit(solution)/shard_map/attend_forward/pallas_call | solution.py:105
  159.8 3.7 all-to-all-start.1
  164.0 14.7 %all-to-all-done.1 = bf16[8,256,128]{2,1,0:T(8,128)(2,1)S(1)} async-done(((bf16[8,256,128]{2,1,0:T(8,128)(2,1)}), bf16[8,256,128]{2,1,0:T(8,128)(2,1)S(1)}, u32[]{:S(2)}, u32[]{:S(2)}) %all-to-all-start.1) | async-done | bytes 524320 | tf_op jit(solution)/shard_map/all_to_all | solution.py:212
  178.6 0.8 copy-done.12
  179.4 1.2 copy.40
  180.7 2.7 fusion.32
  183.4 1.0 copy-done
  184.6 43.5 %all-gather.11.cloned.1.call-done = bf16[1024,4096]{1,0:T(8,128)(2,1)} async-done(((bf16[32,4096]{1,0:T(8,128)(2,1)}), bf16[1024,4096]{1,0:T(8,128)(2,1)}) %all-gather.11.cloned.1.call-update) | async-done | bytes 8388624 | tf_op jit(solution)/shard_map/all_gather | solution.py:216
  228.1 7.3 multiply_convert_fusion
  235.3 71.6 %all-gather.13.cloned.1.call-done = bf16[4096,1024]{1,0:T(8,128)(2,1)} async-done(((bf16[128,1024]{1,0:T(8,128)(2,1)}), bf16[4096,1024]{1,0:T(8,128)(2,1)}) %all-gather.13.cloned.1.call-update) | async-done | bytes 8388624 | tf_op jit(solution)/shard_map/all_gather | solution.py:216
  306.9 6.7 fusion.33
  314.5 1.3 fusion.29
  315.9 6.8 convert_reduce_fusion
  322.8 2.7 multiply_reduce_fusion
  325.9 1.0 copy-done.3
  326.9 0.7 convolution_convert_fusion.3
  327.6 1.0 copy.41
  328.6 2.0 copy.42
  330.7 4.1 all-to-all-start.2
  335.0 3.4 convolution_convert_fusion.2
  338.5 11.8 %all-to-all-done.2.grad_ref = bf16[8,256,128]{2,1,0:T(8,128)(2,1)S(1)} async-done(((bf16[8,256,128]{2,1,0:T(8,128)(2,1)}), bf16[8,256,128]{2,1,0:T(8,128)(2,1)S(1)}, u32[]{:S(2)}, u32[]{:S(2)}) %all-to-all-start.2) | async-done | bytes 524320 | tf_op jit(solution)/shard_map/all_to_all | solution.py:212
  350.4 23.8 %attend_backward.1 = bf16[8,3,256,128]{3,2,1,0:T(8,128)(2,1)S(1)} custom-call(bf16[8,3,256,128]{3,2,1,0:T(8,128)(2,1)S(1)} %all_to_all.20.q_ref.k_ref.v_ref, bf16[8,3,256,128]{3,2,1,0:T(8,128)(2,1)S(1)} %all_to_all.20.q_ref.k_ref.v_ref, bf16[8,3,256,128]{3,2,1,0:T(8,128)(2,1)S(1)} %all_to_all.20.q_ref.k_ref.v_ref, ...), custom_call_target="tpu_custom_call" | custom-call | flops 21474836480 | bytes 5242880 | tf_op jit(solution)/shard_map/attend_backward/pallas_call | solution.py:183
  374.1 47.3 %all_to_all.21 = bf16[8,3,256,128]{3,2,1,0:T(8,128)(2,1)S(1)} all-to-all(bf16[8,3,256,128]{3,2,1,0:T(8,128)(2,1)S(1)} %attend_backward.1), channel_id=1, replica_groups=mesh['dp'=4,'seq'=8] {'seq'}, dimensions={0} | all-to-all | bytes 3145728 | tf_op jit(solution)/shard_map/all_to_all | solution.py:212
  421.4 0.7 copy.43
  422.1 5.5 convert_bitcast_fusion
  427.6 8.6 copy.45
  436.3 1.2 copy-done.2
  437.5 7.3 convolution_convert_fusion.1
  444.9 1.2 copy-done.10
  446.1 7.2 convolution_convert_fusion
  453.3 1.0 copy-done.8
  455.4 39.7 %all-reduce = f32[32,384]{1,0:T(8,128)S(1)} all-reduce(f32[32,384]{1,0:T(8,128)S(1)} %concatenate.11), channel_id=4, replica_groups=mesh['dp'=4,'seq'=8] {'dp','seq'}, use_global_device_ids=true, to_apply=%region_18.0.clone | all-reduce | flops 12288 | bytes 98304
  496.3 5.8 fusion.12
  502.1 1.5 convert_element_type.210
  503.6 93.0 %reduce-scatter.13.cloned.1.call-done = bf16[32,3072]{1,0:T(8,128)(2,1)} async-done(((bf16[1024,3072]{1,0:T(8,128)(2,1)}), bf16[32,3072]{1,0:T(8,128)(2,1)}) %reduce-scatter.13.cloned.1.call-update) | async-done | bytes 196624
  596.6 1.3 copy.46
  597.9 1.0 copy.44
  598.9 183.5 %reduce-scatter.9.cloned.1.call-done = bf16[32,4096]{1,0:T(8,128)(2,1)} async-done(((bf16[1024,4096]{1,0:T(8,128)(2,1)}), bf16[32,4096]{1,0:T(8,128)(2,1)}) %reduce-scatter.9.cloned.1.call-update) | async-done | bytes 262160 | tf_op jit(solution)/shard_map/reduce_scatter | solution.py:220
  782.4 1.8 convert_element_type.212
  784.2 184.6 %reduce-scatter.11.cloned.1.call-done = bf16[128,1024]{1,0:T(8,128)(2,1)} async-done(((bf16[4096,1024]{1,0:T(8,128)(2,1)}), bf16[128,1024]{1,0:T(8,128)(2,1)}) %reduce-scatter.11.cloned.1.call-update) | async-done | bytes 262160 | tf_op jit(solution)/shard_map/reduce_scatter | solution.py:220
  968.7 1.8 convert_element_type.214
  (84 shorter events, 7.2 us)
Async XLA Ops:
  7.2 80.0 %all-gather.7.cloned.1.call-start = ((), (), s32[]{:S(2)}) async-start(), calls=%async_computation.8 | async-start | bytes 6488064 | tf_op jit(solution)/shard_map/all_gather | solution.py:216
  7.9 172.8 %all-gather.9.cloned.1.call-start = ((), (), s32[]{:S(2)}) async-start(), calls=%async_computation.9 | async-start | bytes 2162688 | tf_op jit(solution)/shard_map/all_gather | solution.py:216
  8.7 219.4 %all-gather.11.cloned.1.call-start = ((), (), s32[]{:S(2)}) async-start(), calls=%async_computation.10 | async-start | bytes 8650752 | tf_op jit(solution)/shard_map/all_gather | solution.py:216
  9.4 297.5 %all-gather.13.cloned.1.call-start = ((), (), s32[]{:S(2)}) async-start(), calls=%async_computation.11 | async-start | bytes 8650752 | tf_op jit(solution)/shard_map/all_gather | solution.py:216
  159.8 18.9 %all-to-all-start.1 = ((bf16[8,256,128]{2,1,0:T(8,128)(2,1)}), bf16[8,256,128]{2,1,0:T(8,128)(2,1)S(1)}, u32[]{:S(2)}, u32[]{:S(2)}) async-start(bf16[8,256,128]{2,1,0:T(8,128)(2,1)} %get-tuple-element.18), calls=%async_computation.1 | async-start | bytes 1048576 | tf_op jit(solution)/shard_map/all_to_all | solution.py:212
  178.6 0.8 copy-start.12
  180.7 54.7 %copy-start.6 = (bf16[256,8,128]{0,2,1:T(8,128)(2,1)}, bf16[256,8,128]{0,2,1:T(8,128)(2,1)S(1)}, u32[]{:S(2)}) copy-start(bf16[256,8,128]{0,2,1:T(8,128)(2,1)S(1)} %copy.40) | copy-start | bytes 1572868
  183.4 1.0 copy-start
  306.9 7.0 copy-start.7
  313.7 2.2 copy-start.13
  314.5 8.2 slice-start
  315.8 6.9 copy-start.9
  315.9 6.8 copy-start.1
  315.9 6.9 slice-start.1
  322.7 2.8 copy-start.11
  322.7 4.1 copy-start.5
  325.9 1.0 copy-start.3
  330.7 19.7 %all-to-all-start.2 = ((bf16[8,256,128]{2,1,0:T(8,128)(2,1)}), bf16[8,256,128]{2,1,0:T(8,128)(2,1)S(1)}, u32[]{:S(2)}, u32[]{:S(2)}) async-start(bf16[8,256,128]{2,1,0:T(8,128)(2,1)} %bitcast.96), calls=%async_computation.2 | async-start | bytes 1048576 | tf_op jit(solution)/shard_map/all_to_all | solution.py:212
  334.8 167.4 %reduce-scatter.7.cloned.1.call-start = ((), (), s32[]{:S(2)}) async-start(), calls=%async_computation.12 | async-start | bytes 2162688 | tf_op jit(solution)/shard_map/reduce_scatter | solution.py:220
  338.5 258.1 %reduce-scatter.13.cloned.1.call-start = ((), (), s32[]{:S(2)}) async-start(), calls=%async_computation.15 | async-start | bytes 6488064
  436.3 1.2 copy-start.2
  436.3 346.1 %reduce-scatter.9.cloned.1.call-start = ((), (), s32[]{:S(2)}) async-start(), calls=%async_computation.13 | async-start | bytes 8650752 | tf_op jit(solution)/shard_map/reduce_scatter | solution.py:220
  444.8 1.2 copy-start.10
  444.9 523.9 %reduce-scatter.11.cloned.1.call-start = ((), (), s32[]{:S(2)}) async-start(), calls=%async_computation.14 | async-start | bytes 8650752 | tf_op jit(solution)/shard_map/reduce_scatter | solution.py:220
  453.3 1.0 copy-start.8
  453.3 43.1 %copy-start.4 = (f32[256,1024]{1,0:T(8,128)S(1)}, f32[256,1024]{1,0:T(8,128)}, u32[]{:S(2)}) copy-start(f32[256,1024]{1,0:T(8,128)} %copy-done.3) | copy-start | bytes 3145732
Sparse Core Ops, SparseCore 0:
  10.9 72.3 all-gather.6
  86.3 59.0 all-gather.8
  148.3 79.6 all-gather.10
  230.9 75.9 all-gather.12
  338.6 140.3 reduce-scatter.6
  485.4 111.1 reduce-scatter.12
  598.9 183.4 reduce-scatter.8
  784.7 183.9 reduce-scatter.10

commit v2 on v1

--- a/solution.py
+++ b/solution.py
@@ -212,12 +212,59 @@
     return lax.all_to_all(blocks, "seq", 0, 0, tiled=True)
 
 
-def gather(shard):
-    return lax.all_gather(shard, AXES, axis=0, tiled=True)
-
-
-def scatter(whole):
-    return lax.psum_scatter(whole, AXES, scatter_dimension=0, tiled=True)
+def bit_order(turn):
+    low = (lax.axis_size("seq") - 1).bit_length()
+    bits = low + (lax.axis_size("dp") - 1).bit_length()
+    near = [bits - 1, 0, 1]
+    near = near[turn:] + near[:turn]
+    return [low] + near + [bit for bit in range(bits) if bit != low and bit not in near]
+
+
+def my_bit(bit):
+    index = lax.axis_index("dp") * lax.axis_size("seq") + lax.axis_index("seq")
+    return lax.rem(lax.div(index, 1 << bit), 2)
+
+
+def exchange(block, bit):
+    devices = lax.axis_size("dp") * lax.axis_size("seq")
+    return lax.ppermute(block, AXES, [(i, i ^ (1 << bit)) for i in range(devices)])
+
+
+def gather(shard, turn):
+    block = shard
+    held = []
+    for bit in reversed(bit_order(turn)):
+        other = exchange(block, bit)
+        upper = my_bit(bit) == 1
+        axis = sum(1 for have in held if have > bit)
+        block = jnp.stack(
+            [jnp.where(upper, other, block), jnp.where(upper, block, other)], axis=axis
+        )
+        held.append(bit)
+    return block.reshape((-1,) + shard.shape[1:])
+
+
+def scatter(whole, turn):
+    order = bit_order(turn)
+    kind = whole.dtype
+    block = whole.reshape((2,) * len(order) + whole.shape[1:])
+    held = sorted(order, reverse=True)
+    for bit in order:
+        axis = held.index(bit)
+        mine = my_bit(bit)
+        kept = lax.dynamic_index_in_dim(block, mine, axis, keepdims=False)
+        sent = lax.dynamic_index_in_dim(block, 1 - mine, axis, keepdims=False)
+        other = exchange(sent, bit)
+        held.remove(bit)
+        block = kept.astype(jnp.float32) + other.astype(jnp.float32)
+        if held:
+            block = block.astype(kind)
+    return block
+
+
+def scatter_rows(grad, turn):
+    devices = lax.axis_size("dp") * lax.axis_size("seq")
+    return scatter(grad.astype(jnp.bfloat16).reshape(devices, -1, grad.shape[1]), turn)
 
 
 def per_device(
@@ -240,11 +287,11 @@
     groups = lax.axis_size("seq")
     devices = lax.axis_size("dp") * groups
     vectors = (bias_q, bias_v, bias_out, gain_one, shift_one, bias_in, bias_back, gain_two, shift_two)
-    wide_qkv = gather(w_qkv)
-    rows_of = lax.all_gather(jnp.concatenate(vectors), AXES, axis=0, tiled=False)
-    wide_out = gather(w_out)
-    wide_in = gather(w_in)
-    wide_back = gather(w_back)
+    wide_qkv = [gather(w_qkv[:, part * D : (part + 1) * D], part) for part in range(3)]
+    rows_of = gather(jnp.concatenate(vectors)[None], 0)
+    wide_out = gather(w_out, 2)
+    wide_in = gather(w_in, 1)
+    wide_back = gather(w_back, 0)
     full = []
     place = 0
     for vector in vectors:
@@ -256,9 +303,14 @@
     sequence = inputs[0]
     rows_here = sequence.shape[0]
     width = D // groups
-    bias_qkv = jnp.concatenate([full_bq, jnp.zeros_like(full_bq), full_bv], axis=1)
-    projected = (dense(sequence, wide_qkv) + bias_qkv).astype(jnp.bfloat16)
-    packed = swap(jnp.transpose(projected.reshape(rows_here, 3, groups, width), (2, 1, 0, 3)))
+    projected = jnp.stack(
+        [
+            (dense(sequence, wide_qkv[0]) + full_bq).astype(jnp.bfloat16),
+            dense(sequence, wide_qkv[1]).astype(jnp.bfloat16),
+            (dense(sequence, wide_qkv[2]) + full_bv).astype(jnp.bfloat16),
+        ]
+    )
+    packed = swap(jnp.transpose(projected.reshape(3, rows_here, groups, width), (2, 0, 1, 3)))
     att_low, att_full, lse = attend_forward(packed)
     attended = jnp.transpose(swap(att_low), (1, 0, 2)).reshape(rows_here, D)
 
@@ -278,25 +330,29 @@
     grad_result = norm_back(grad_rows, normed_two, inv_two, full_g2)
     grad_bias_back = jnp.sum(grad_result, axis=0)
     result_low = grad_result.astype(jnp.bfloat16)
-    own_back = scatter(dense_left_t(gated, result_low).astype(jnp.bfloat16))
+    own_back = scatter_rows(dense_left_t(gated, result_low), 0)
     grad_inner = (dense_right_t(result_low, wide_back) * gelu_slope(inner)).astype(jnp.bfloat16)
     grad_bias_in = jnp.sum(grad_inner.astype(jnp.float32), axis=0)
-    own_in = scatter(dense_left_t(first_low, grad_inner).astype(jnp.bfloat16))
+    own_in = scatter_rows(dense_left_t(first_low, grad_inner), 1)
     grad_first = grad_result + dense_right_t(grad_inner, wide_in)
     grad_gain_one = jnp.sum(grad_first * normed_one, axis=0)
     grad_shift_one = jnp.sum(grad_first, axis=0)
     grad_hidden = norm_back(grad_first, normed_one, inv_one, full_g1)
     grad_bias_out = jnp.sum(grad_hidden, axis=0)
     hidden_low = grad_hidden.astype(jnp.bfloat16)
-    own_out = scatter(dense_left_t(attended, hidden_low).astype(jnp.bfloat16))
+    own_out = scatter_rows(dense_left_t(attended, hidden_low), 2)
     grad_att = dense_right_t(hidden_low, wide_out).astype(jnp.bfloat16)
     grad_heads = swap(jnp.transpose(grad_att.reshape(rows_here, groups, width), (1, 0, 2)))
     grad_packed = swap(attend_backward(packed, grad_heads, att_full, lse))
-    grad_proj = jnp.transpose(grad_packed, (2, 1, 0, 3)).reshape(rows_here, 3 * D)
-    own_qkv = scatter(dense_left_t(sequence, grad_proj).astype(jnp.bfloat16))
-    grad_bias_q = jnp.sum(grad_proj[:, :D].astype(jnp.float32), axis=0)
-    grad_bias_v = jnp.sum(grad_proj[:, 2 * D :].astype(jnp.float32), axis=0)
-    input_grad = grad_hidden + dense_right_t(grad_proj, wide_qkv)
+    grad_proj = jnp.transpose(grad_packed, (1, 2, 0, 3)).reshape(3, rows_here, D)
+    own_qkv = jnp.concatenate(
+        [scatter_rows(dense_left_t(sequence, grad_proj[part]), part) for part in range(3)], axis=1
+    )
+    grad_bias_q = jnp.sum(grad_proj[0].astype(jnp.float32), axis=0)
+    grad_bias_v = jnp.sum(grad_proj[2].astype(jnp.float32), axis=0)
+    input_grad = grad_hidden + sum(
+        dense_right_t(grad_proj[part], wide_qkv[part]) for part in range(3)
+    )
 
     sums = (
         grad_bias_q,
@@ -309,12 +365,9 @@
         grad_gain_two,
         grad_shift_two,
     )
-    owned = lax.psum_scatter(
-        jnp.concatenate([item.reshape(devices, -1) for item in sums], axis=1),
-        AXES,
-        scatter_dimension=0,
-        tiled=False,
-    )
+    owned = scatter(
+        jnp.concatenate([item.reshape(devices, -1) for item in sums], axis=1)[:, None], 0
+    )[0]
     small = []
     place = 0
     for vector in vectors:
@@ -324,16 +377,16 @@
     return (
         mixed[None],
         input_grad[None],
-        own_qkv.astype(jnp.float32),
+        own_qkv,
         own_bq,
         own_bv,
-        own_out.astype(jnp.float32),
+        own_out,
         own_bo,
         own_g1,
         own_s1,
-        own_in.astype(jnp.float32),
+        own_in,
         own_b1,
-        own_back.astype(jnp.float32),
+        own_back,
         own_b2,
         own_g2,
         own_s2,

time: 979 us -> 599 us (0.61)
  waiting for transfers between devices: 605 us -> 261 us
  blocking collectives: 202 us -> 0 us
  starting transfers between devices: 8.33 us -> 85.8 us
  other arithmetic: 8.37 us -> 80.1 us
  local copies, waits for them, and re-layouts: 32.3 us -> 57.3 us
  between operations: 14.5 us -> 2.76 us
    reduce_scatter x3 -> x0, waiting for transfers between devices: 368 us -> none  [scatter(): return lax.psum_scatter(whole, AXES, scatter_dimension=0, tiled=True)]
    ppermute x0 -> x70, waiting for transfers between devices: none -> 247 us  [exchange(): lax.ppermute(block, AXES, [(i, i ^ 1 << bit) for i in range(devices)])]
    all_gather x4 -> x0, waiting for transfers between devices: 115 us -> none  [gather(): return lax.all_gather(shard, AXES, axis=0, tiled=True)]
    unnamed x9 -> x0, waiting for transfers between devices: 95.6 us -> none
    all_to_all x2 -> x0, blocking collectives: 91.3 us -> none  [swap(): return lax.all_to_all(blocks, 'seq', 0, 0, tiled=True)]
    all_gather x1 -> x0, blocking collectives: 70.8 us -> none  [per_device(): lax.all_gather(jnp.concatenate(vectors), AXES, axis=0, tiled=False)]
    ppermute x0 -> x70, starting transfers between devices: none -> 67.1 us  [exchange(): lax.ppermute(block, AXES, [(i, i ^ 1 << bit) for i in range(devices)])]
    another operation x0 -> x69, other arithmetic: none -> 55.1 us  [gather(): jnp.stack([jnp.where(upper, other, block), jnp.where(upper, block, other)...]
  transfers between devices with their start and end apart: 10 -> 74, of which waited for: 7 -> 40; matrix products, arithmetic and copies ran while one was open for 7% -> 24% of each run, Pallas kernels for 5% -> 8%
where the time goes in v2:
time: 599 us; the launch traced here: 590 us
  waiting for transfers between devices  261 us (44%)
  starting transfers between devices  85.8 us (14%)
  other arithmetic  80.1 us (13%)
  local copies, waits for them, and re-layouts  57.3 us (10%)
  matrix products  56.3 us (9%)
  Pallas kernels  47 us (8%)
    ppermute x70, waiting for transfers between devices, exchange(): lax.ppermute(block, AXES, [(i, i ^ 1 << bit) for i in range(devices)])  247 us
    ppermute x70, starting transfers between devices, exchange(): lax.ppermute(block, AXES, [(i, i ^ 1 << bit) for i in range(devices)])  67.1 us
    another operation x69, other arithmetic, gather(): jnp.stack([jnp.where(upper, other, block), jnp.where(upper, block, other)...  55.1 us
    pallas_call x1, Pallas kernels, attend_backward(): pl.pallas_call(attend_backward_body, grid=(groups,), in_specs=[pl.BlockSp...  24.9 us
    dot_general x6, matrix products, dense_right_t(): lax.dot_general(left, right, (((1,), (1,)), ((), ())), preferred_element_...  23.2 us
    pallas_call x1, Pallas kernels, attend_forward(): pl.pallas_call(attend_forward_body, grid=(groups,), in_specs=[pl.BlockSpe...  22.2 us
    all_to_all x4, starting transfers between devices, swap(): return lax.all_to_all(blocks, 'seq', 0, 0, tiled=True)  18.7 us
    dot_general x6, matrix products, dense_left_t(): lax.dot_general(left, right, (((0,), (0,)), ((), ())), preferred_element_...  17.6 us
  transfers between devices with their start and end apart: 74, of which 40 were waited for; matrix products, arithmetic and copies ran while one was open for 24% of the time, Pallas kernels for 8%

profile of v2, /device:TPU:0, one launch (start us, length us, event | category | flops | bytes accessed | tf_op | source)
XLA Modules:
  0.0 590.0 jit_solution(8056291097228582968)
XLA Ops:
  0.7 6.1 %concatenate.29 = bf16[384]{0:T(512)(128)(2,1)S(1)} concatenate(bf16[32]{0:T(256)(128)(2,1)} %param.18, bf16[32]{0:T(256)(128)(2,1)} %param.19, bf16[32]{0:T(256)(128)(2,1)} %param.21, bf16[32]{0:T(256)(128)(2,1)} %param.22, bf16[32]{0:T(256)(128)(2,1)} %param.23, bf16[128]{0:T(256)(128)(2,1)} %param.25, bf16[32]{0:T(256)(128)(2,1)} %param.27, bf16[32]{0:T(256)(128)(2,1)} %param.28, ...), dimensions={0} | concatenate | bytes 1536 | tf_op jit(solution)/shard_map/concatenate | solution.py:291
  6.8 4.1 collective-permute-start.5
  24.5 2.9 collective-permute-start
  27.5 2.9 collective-permute-start.25
  30.8 15.4 %collective-permute-done.20 = bf16[32,1024]{1,0:T(8,128)(2,1)S(1)} collective-permute-done((bf16[32,1024]{1,0:T(8,128)(2,1)}, bf16[32,1024]{1,0:T(8,128)(2,1)S(1)}, u32[]{:S(2)}, u32[]{:S(2)}) %collective-permute-start.20) | collective-permute-done | bytes 65568 | tf_op jit(solution)/shard_map/ppermute | solution.py:230
  49.6 2.9 collective-permute-start.10
  52.5 9.1 %collective-permute-done.15 = bf16[32,1024]{1,0:T(8,128)(2,1)S(1)} collective-permute-done((bf16[32,1024]{1,0:T(8,128)(2,1)S(1)}, bf16[32,1024]{1,0:T(8,128)(2,1)S(1)}, u32[]{:S(2)}, u32[]{:S(2)}) %collective-permute-start.15) | collective-permute-done | bytes 65568 | tf_op jit(solution)/shard_map/ppermute | solution.py:230
  84.6 8.6 %collective-permute-done.26 = bf16[2,32,4096]{2,1,0:T(8,128)(2,1)S(1)} collective-permute-done((bf16[2,32,4096]{2,1,0:T(8,128)(2,1)S(1)}, bf16[2,32,4096]{2,1,0:T(8,128)(2,1)S(1)}, u32[]{:S(2)}, u32[]{:S(2)}) %collective-permute-start.26) | collective-permute-done | bytes 524320 | tf_op jit(solution)/shard_map/ppermute | solution.py:230
  95.4 7.4 %collective-permute-done.3 = bf16[2,2,2,32,1024]{4,3,2,1,0:T(8,128)(2,1)S(1)} collective-permute-done((bf16[2,2,2,32,1024]{4,3,2,1,0:T(8,128)(2,1)S(1)}, bf16[2,2,2,32,1024]{4,3,2,1,0:T(8,128)(2,1)S(1)}, u32[]{:S(2)}, u32[]{:S(2)}) %collective-permute-start.3) | collective-permute-done | bytes 524320 | tf_op jit(solution)/shard_map/ppermute | solution.py:230
  103.6 11.6 %collective-permute-done.18 = bf16[2,2,2,32,1024]{4,3,1,2,0:T(8,128)(2,1)S(1)} collective-permute-done((bf16[2,2,2,32,1024]{4,3,1,2,0:T(8,128)(2,1)S(1)}, bf16[2,2,2,32,1024]{4,3,1,2,0:T(8,128)(2,1)S(1)}, u32[]{:S(2)}, u32[]{:S(2)}) %collective-permute-start.18) | collective-permute-done | bytes 524320 | tf_op jit(solution)/shard_map/ppermute | solution.py:230
  118.2 16.6 %collective-permute-done.27 = bf16[2,2,32,4096]{3,2,1,0:T(8,128)(2,1)S(1)} collective-permute-done((bf16[2,2,32,4096]{3,2,1,0:T(8,128)(2,1)S(1)}, bf16[2,2,32,4096]{3,2,1,0:T(8,128)(2,1)S(1)}, u32[]{:S(2)}, u32[]{:S(2)}) %collective-permute-start.27) | collective-permute-done | bytes 1048608 | tf_op jit(solution)/shard_map/ppermute | solution.py:230
  144.3 3.2 select_bitcast_fusion.15
  156.9 6.3 %all-to-all-start = ((bf16[8,3,256,128]{3,2,1,0:T(8,128)(2,1)}), bf16[8,3,256,128]{3,2,1,0:T(8,128)(2,1)S(1)}, u32[]{:S(2)}, u32[]{:S(2)}) async-start(bf16[8,3,256,128]{3,2,1,0:T(8,128)(2,1)} %maximum_bitcast_fusion), calls=%async_computation | async-start | bytes 3145728 | tf_op jit(solution)/shard_map/all_to_all | solution.py:212
  163.3 35.1 %collective-permute-done.28 = bf16[2,2,2,32,4096]{4,3,2,1,0:T(8,128)(2,1)} collective-permute-done((bf16[2,2,2,32,4096]{4,3,2,1,0:T(8,128)(2,1)}, bf16[2,2,2,32,4096]{4,3,2,1,0:T(8,128)(2,1)}, u32[]{:S(2)}, u32[]{:S(2)}) %collective-permute-start.28) | collective-permute-done | bytes 2097184 | tf_op jit(solution)/shard_map/ppermute | solution.py:230
  200.8 2.6 pad_maximum_fusion.2
  209.0 2.6 pad_maximum_fusion.3
  212.4 22.2 %attend_forward.1 = (bf16[8,256,128]{2,1,0:T(8,128)(2,1)}, f32[8,256,128]{2,1,0:T(8,128)S(1)}, f32[8,2,256]{2,1,0:T(2,128)S(1)}) custom-call(bf16[8,3,256,128]{3,2,1,0:T(8,128)(2,1)S(1)} %all-to-all-done.q_ref.k_ref.v_ref, bf16[8,3,256,128]{3,2,1,0:T(8,128)(2,1)S(1)} %all-to-all-done.q_ref.k_ref.v_ref, ...), custom_call_target="tpu_custom_call" | custom-call | flops 8589934592 | bytes 2621440 | tf_op jit(solution)/shard_map/attend_forward/pallas_call | solution.py:105
  234.5 4.7 all-to-all-start.1
  243.1 11.3 %all-to-all-done.1 = bf16[8,256,128]{2,1,0:T(8,128)(2,1)} async-done(((bf16[8,256,128]{2,1,0:T(8,128)(2,1)}), bf16[8,256,128]{2,1,0:T(8,128)(2,1)}, u32[]{:S(2)}, u32[]{:S(2)}) %all-to-all-start.1) | async-done | bytes 524320 | tf_op jit(solution)/shard_map/all_to_all | solution.py:212
  256.5 2.7 fusion.86
  259.5 5.3 select_bitcast_fusion.3
  264.8 7.7 %pad_maximum_fusion = bf16[2,2,2,2,2,32,4096]{6,5,4,3,2,1,0:T(8,128)(2,1)} fusion(bf16[2,1,2,2,2,32,4096]{6,5,4,3,2,1,0:T(8,128)(2,1)} %get-tuple-element.41, bf16[2,1,2,2,2,32,4096]{6,5,4,3,2,1,0:T(8,128)(2,1)} %get-tuple-element.40), kind=kLoop, calls=%fused_computation | loop fusion | flops 4194304 | bytes 16777216 | tf_op jit(solution)/shard_map/stack | solution.py:240
  272.5 5.5 select_bitcast_fusion.1
  278.0 7.5 %pad_maximum_fusion.1 = bf16[2,2,2,2,2,128,1024]{6,5,4,3,2,1,0:T(8,128)(2,1)} fusion(bf16[2,1,2,2,2,128,1024]{6,5,4,3,2,1,0:T(8,128)(2,1)} %get-tuple-element.39, bf16[2,1,2,2,2,128,1024]{6,5,4,3,2,1,0:T(8,128)(2,1)} %get-tuple-element.38), kind=kLoop, calls=%fused_computation.1 | loop fusion | flops 4194304 | bytes 16777216 | tf_op jit(solution)/shard_map/stack | solution.py:240
  285.5 5.5 multiply_convert_fusion
  296.0 12.7 %convert_reduce_fusion = (f32[4096]{0:T(1024)S(1)}, bf16[256,4096]{1,0:T(8,128)(2,1)S(1)}) fusion(f32[256,4096]{1,0:T(8,128)S(1)} %get-tuple-element.141, bf16[4096,1024]{1,0:T(8,128)(2,1)S(1)} %bitcast.511, f32[256,1024]{1,0:T(8,128)S(1)} %get-tuple-element.31), kind=kOutput, calls=%fused_computation.26 | convolution fusion | flops 2160324608 | bytes 15745024 | tf_op jit(solution)/shard_map/dot_general | solution.py:60
  308.8 2.8 multiply_reduce_fusion
  315.8 2.7 convolution_convert_fusion.6
  321.5 3.7 all-to-all-start.2
  325.2 7.8 %convolution_convert_fusion.1 = bf16[1024,4096]{1,0:T(8,128)(2,1)} fusion(bf16[256,4096]{1,0:T(8,128)(2,1)} %copy-done.44, f32[256,1024]{1,0:T(8,128)} %copy-done.1, f32[1024]{0:T(1024)S(1)} %reshape.315, f32[1024]{0:T(1024)S(1)} %reshape.314, f32[256]{0:T(256)S(1)} %add_rsqrt_fusion.1, f32[256]{0:T(256)S(1)} %broadcast_multiply_fusion.5), kind=kOutput, calls=%fused_computation.7 | convolution fusion | flops 2152988672 | bytes 11544576 | tf_op jit(solution)/shard_map/dot_general | solution.py:54
  337.9 2.6 all-to-all-done.2.grad_ref
  340.5 24.9 %attend_backward.1 = bf16[8,3,256,128]{3,2,1,0:T(8,128)(2,1)} custom-call(bf16[8,3,256,128]{3,2,1,0:T(8,128)(2,1)S(1)} %all-to-all-done.q_ref.k_ref.v_ref, bf16[8,3,256,128]{3,2,1,0:T(8,128)(2,1)S(1)} %all-to-all-done.q_ref.k_ref.v_ref, bf16[8,3,256,128]{3,2,1,0:T(8,128)(2,1)S(1)} %all-to-all-done.q_ref.k_ref.v_ref, ...), custom_call_target="tpu_custom_call" | custom-call | flops 21474836480 | bytes 5242880 | tf_op jit(solution)/shard_map/attend_backward/pallas_call | solution.py:183
  365.4 3.9 all-to-all-start.3
  371.2 8.0 %constant_dynamic-slice_fusion.3 = (bf16[2,1,2,2,2,32,4096]{6,5,4,3,2,1,0:T(8,128)(2,1)}, bf16[2,1,2,2,2,32,4096]{6,5,4,3,2,1,0:T(8,128)(2,1)}) fusion(bf16[2,2,2,2,2,32,4096]{6,5,4,3,2,1,0:T(8,128)(2,1)} %bitcast.495, s32[]{:T(128)S(6)} %select_n.582, s32[]{:T(128)S(6)} %select_n.583), kind=kLoop, calls=%fused_computation.258 | loop fusion | bytes 16777224 | tf_op jit(solution)/shard_map/jit(dynamic_index_in_dim)/dynamic_slice | solution.py:255
  381.3 5.7 convolution_convert_fusion
  387.5 5.0 copy.134
  394.9 3.5 constant_dynamic-slice_fusion.1
  398.4 2.7 copy.133
  401.3 7.7 %collective-permute-done.59 = bf16[32,1024]{1,0:T(8,128)(2,1)S(1)} collective-permute-done((bf16[32,1024]{1,0:T(8,128)(2,1)S(1)}, bf16[32,1024]{1,0:T(8,128)(2,1)S(1)}, u32[]{:S(2)}, u32[]{:S(2)}) %collective-permute-start.59) | collective-permute-done | bytes 65568 | tf_op jit(solution)/shard_map/ppermute | solution.py:230
  439.2 3.7 fusion.1
  445.1 4.3 fusion
  456.0 8.8 %collective-permute-done.46 = bf16[2,2,2,32,1024]{4,3,1,2,0:T(8,128)(2,1)S(1)} collective-permute-done((bf16[2,2,2,32,1024]{4,3,1,2,0:T(8,128)(2,1)S(1)}, bf16[2,2,2,32,1024]{4,3,1,2,0:T(8,128)(2,1)S(1)}, u32[]{:S(2)}, u32[]{:S(2)}) %collective-permute-start.46) | collective-permute-done | bytes 524320 | tf_op jit(solution)/shard_map/ppermute | solution.py:230
  466.6 42.7 %collective-permute-done.36 = bf16[2,2,2,32,1024]{4,3,0,1,2:T(8,128)(2,1)S(1)} collective-permute-done((bf16[2,2,2,32,1024]{4,3,0,1,2:T(8,128)(2,1)S(1)}, bf16[2,2,2,32,1024]{4,3,0,1,2:T(8,128)(2,1)S(1)}, u32[]{:S(2)}, u32[]{:S(2)}) %collective-permute-start.36) | collective-permute-done | bytes 524320 | tf_op jit(solution)/shard_map/ppermute | solution.py:230
  511.5 3.1 collective-permute-done.47
  533.3 18.7 %collective-permute-done.62 = bf16[2,2,32,4096]{3,2,1,0:T(8,128)(2,1)S(1)} collective-permute-done((bf16[2,2,32,4096]{3,2,1,0:T(8,128)(2,1)S(1)}, bf16[2,2,32,4096]{3,2,1,0:T(8,128)(2,1)S(1)}, u32[]{:S(2)}, u32[]{:S(2)}) %collective-permute-start.62) | collective-permute-done | bytes 1048608 | tf_op jit(solution)/shard_map/ppermute | solution.py:230
  555.9 9.2 %collective-permute-done.63 = bf16[2,32,4096]{2,1,0:T(8,128)(2,1)S(1)} collective-permute-done((bf16[2,32,4096]{2,1,0:T(8,128)(2,1)S(1)}, bf16[2,32,4096]{2,1,0:T(8,128)(2,1)S(1)}, u32[]{:S(2)}, u32[]{:S(2)}) %collective-permute-start.63) | collective-permute-done | bytes 524320 | tf_op jit(solution)/shard_map/ppermute | solution.py:230
  568.8 15.1 %collective-permute-done.64 = bf16[32,4096]{1,0:T(8,128)(2,1)S(1)} collective-permute-done((bf16[32,4096]{1,0:T(8,128)(2,1)S(1)}, bf16[32,4096]{1,0:T(8,128)(2,1)S(1)}, u32[]{:S(2)}, u32[]{:S(2)}) %collective-permute-start.64) | collective-permute-done | bytes 262176 | tf_op jit(solution)/shard_map/ppermute | solution.py:230
  584.7 4.0 collective-permute-done.69
  (426 shorter events, 174.0 us)
Async XLA Ops:
  24.5 24.1 %collective-permute-start = (bf16[32,1024]{1,0:T(8,128)(2,1)S(1)}, bf16[32,1024]{1,0:T(8,128)(2,1)S(1)}, u32[]{:S(2)}, u32[]{:S(2)}) collective-permute-start(bf16[32,1024]{1,0:T(8,128)(2,1)S(1)} %slice.107), channel_id=1, source_target_pairs={{0,4},{1,5},{2,6},{3,7},{4,0},{5,1},{6,2},{7,3},{8,12},{9,13},{10,... | collective-permute-start | bytes 196616 | tf_op jit(solution)/shard_map/ppermute | solution.py:230
  27.5 18.8 %collective-permute-start.20 = (bf16[32,1024]{1,0:T(8,128)(2,1)}, bf16[32,1024]{1,0:T(8,128)(2,1)S(1)}, u32[]{:S(2)}, u32[]{:S(2)}) collective-permute-start(bf16[32,1024]{1,0:T(8,128)(2,1)} %param.20), channel_id=1, source_target_pairs={{0,4},{1,5},{2,6},{3,7},{4,0},{5,1},{6,2},{7,3},{8,12},{9,13},{10,... | collective-permute-start | bytes 196616 | tf_op jit(solution)/shard_map/ppermute | solution.py:230
  27.5 44.8 %collective-permute-start.25 = (bf16[32,4096]{1,0:T(8,128)(2,1)}, bf16[32,4096]{1,0:T(8,128)(2,1)S(1)}, u32[]{:S(2)}, u32[]{:S(2)}) collective-permute-start(bf16[32,4096]{1,0:T(8,128)(2,1)} %param.24), channel_id=1, source_target_pairs={{0,4},{1,5},{2,6},{3,7},{4,0},{5,1},{6,2},{7,3},{8,12},{9,13},{10,... | collective-permute-start | bytes 786440 | tf_op jit(solution)/shard_map/ppermute | solution.py:230
  30.4 42.9 %collective-permute-start.30 = (bf16[128,1024]{1,0:T(8,128)(2,1)}, bf16[128,1024]{1,0:T(8,128)(2,1)S(1)}, u32[]{:S(2)}, u32[]{:S(2)}) collective-permute-start(bf16[128,1024]{1,0:T(8,128)(2,1)} %param.26), channel_id=1, source_target_pairs={{0,4},{1,5},{2,6},{3,7},{4,0},{5,1},{6,2},{7,3},{8,12},{9,13},{10,... | collective-permute-start | bytes 786440 | tf_op jit(solution)/shard_map/ppermute | solution.py:230
  47.1 17.1 %collective-permute-start.21 = (bf16[2,32,1024]{2,1,0:T(8,128)(2,1)S(1)}, bf16[2,32,1024]{2,1,0:T(8,128)(2,1)S(1)}, u32[]{:S(2)}, u32[]{:S(2)}) collective-permute-start(bf16[2,32,1024]{2,1,0:T(8,128)(2,1)S(1)} %pad_maximum_fusion.30), channel_id=1, source_target_pairs={{0,1},{1,0},{2,3},{3,2},{4,5},{5,4},{6,7},{7,6},{8,9},{9,8},{10,11... | collective-permute-start | bytes 393224 | tf_op jit(solution)/shard_map/ppermute | solution.py:230
  49.5 12.2 %collective-permute-start.15 = (bf16[32,1024]{1,0:T(8,128)(2,1)S(1)}, bf16[32,1024]{1,0:T(8,128)(2,1)S(1)}, u32[]{:S(2)}, u32[]{:S(2)}) collective-permute-start(bf16[32,1024]{1,0:T(8,128)(2,1)S(1)} %get-tuple-element.108), channel_id=1, source_target_pairs={{0,4},{1,5},{2,6},{3,7},{4,0},{5,1},{6,2},{7,3},{8,12},{9,13},{10,... | collective-permute-start | bytes 196616 | tf_op jit(solution)/shard_map/ppermute | solution.py:230
  49.6 12.9 %collective-permute-start.10 = (bf16[32,1024]{1,0:T(8,128)(2,1)S(1)}, bf16[32,1024]{1,0:T(8,128)(2,1)S(1)}, u32[]{:S(2)}, u32[]{:S(2)}) collective-permute-start(bf16[32,1024]{1,0:T(8,128)(2,1)S(1)} %get-tuple-element.109), channel_id=1, source_target_pairs={{0,4},{1,5},{2,6},{3,7},{4,0},{5,1},{6,2},{7,3},{8,12},{9,13},{10,... | collective-permute-start | bytes 196616 | tf_op jit(solution)/shard_map/ppermute | solution.py:230
  72.3 11.3 %collective-permute-start.12 = (bf16[2,2,32,1024]{3,2,1,0:T(8,128)(2,1)S(1)}, bf16[2,2,32,1024]{3,2,1,0:T(8,128)(2,1)S(1)}, u32[]{:S(2)}, u32[]{:S(2)}) collective-permute-start(bf16[2,2,32,1024]{3,2,1,0:T(8,128)(2,1)S(1)} %pad_maximum_fusion.24), channel_id=1, source_target_pairs={{0,2},{1,3},{2,0},{3,1},{4,6},{5,7},{6,4},{7,5},{8,10},{9,11},{10,... | collective-permute-start | bytes 786440 | tf_op jit(solution)/shard_map/ppermute | solution.py:230
  73.3 19.9 %collective-permute-start.26 = (bf16[2,32,4096]{2,1,0:T(8,128)(2,1)S(1)}, bf16[2,32,4096]{2,1,0:T(8,128)(2,1)S(1)}, u32[]{:S(2)}, u32[]{:S(2)}) collective-permute-start(bf16[2,32,4096]{2,1,0:T(8,128)(2,1)S(1)} %pad_maximum_fusion.20), channel_id=1, source_target_pairs={{0,16},{1,17},{2,18},{3,19},{4,20},{5,21},{6,22},{7,23},{8,24},{9,... | collective-permute-start | bytes 1572872 | tf_op jit(solution)/shard_map/ppermute | solution.py:230
  76.4 18.0 %collective-permute-start.31 = (bf16[2,128,1024]{2,1,0:T(8,128)(2,1)S(1)}, bf16[2,128,1024]{2,1,0:T(8,128)(2,1)S(1)}, u32[]{:S(2)}, u32[]{:S(2)}) collective-permute-start(bf16[2,128,1024]{2,1,0:T(8,128)(2,1)S(1)} %pad_maximum_fusion.21), channel_id=1, source_target_pairs={{0,2},{1,3},{2,0},{3,1},{4,6},{5,7},{6,4},{7,5},{8,10},{9,11},{10,... | collective-permute-start | bytes 1572872 | tf_op jit(solution)/shard_map/ppermute | solution.py:230
  78.1 126.0 %collective-permute-start.23 = (bf16[2,2,2,32,1024]{4,3,1,2,0:T(8,128)(2,1)}, bf16[2,2,2,32,1024]{4,3,1,2,0:T(8,128)(2,1)}, u32[]{:S(2)}, u32[]{:S(2)}) collective-permute-start(bf16[2,2,2,32,1024]{4,3,1,2,0:T(8,128)(2,1)} %pad_maximum_fusion.19), channel_id=1, source_target_pairs={{0,2},{1,3},{2,0},{3,1},{4,6},{5,7},{6,4},{7,5},{8,10},{9,11},{10,... | collective-permute-start | bytes 1572872 | tf_op jit(solution)/shard_map/ppermute | solution.py:230
  82.0 20.8 %collective-permute-start.3 = (bf16[2,2,2,32,1024]{4,3,2,1,0:T(8,128)(2,1)S(1)}, bf16[2,2,2,32,1024]{4,3,2,1,0:T(8,128)(2,1)S(1)}, u32[]{:S(2)}, u32[]{:S(2)}) collective-permute-start(bf16[2,2,2,32,1024]{4,3,2,1,0:T(8,128)(2,1)S(1)} %pad_maximum_fusion.16), channel_id=1, source_target_pairs={{0,16},{1,17},{2,18},{3,19},{4,20},{5,21},{6,22},{7,23},{8,24},{9,... | collective-permute-start | bytes 1572872 | tf_op jit(solution)/shard_map/ppermute | solution.py:230
  83.6 31.7 %collective-permute-start.18 = (bf16[2,2,2,32,1024]{4,3,1,2,0:T(8,128)(2,1)S(1)}, bf16[2,2,2,32,1024]{4,3,1,2,0:T(8,128)(2,1)S(1)}, u32[]{:S(2)}, u32[]{:S(2)}) collective-permute-start(bf16[2,2,2,32,1024]{4,3,1,2,0:T(8,128)(2,1)S(1)} %pad_maximum_fusion.18), channel_id=1, source_target_pairs={{0,2},{1,3},{2,0},{3,1},{4,6},{5,7},{6,4},{7,5},{8,10},{9,11},{10,... | collective-permute-start | bytes 1572872 | tf_op jit(solution)/shard_map/ppermute | solution.py:230
  93.2 23.2 %collective-permute-start.13 = (bf16[2,2,2,32,1024]{4,3,1,0,2:T(8,128)(2,1)S(1)}, bf16[2,2,2,32,1024]{4,3,1,0,2:T(8,128)(2,1)S(1)}, u32[]{:S(2)}, u32[]{:S(2)}) collective-permute-start(bf16[2,2,2,32,1024]{4,3,1,0,2:T(8,128)(2,1)S(1)} %pad_maximum_fusion.17), channel_id=1, source_target_pairs={{0,1},{1,0},{2,3},{3,2},{4,5},{5,4},{6,7},{7,6},{8,9},{9,8},{10,11... | collective-permute-start | bytes 1572872 | tf_op jit(solution)/shard_map/ppermute | solution.py:230
  94.4 40.4 %collective-permute-start.27 = (bf16[2,2,32,4096]{3,2,1,0:T(8,128)(2,1)S(1)}, bf16[2,2,32,4096]{3,2,1,0:T(8,128)(2,1)S(1)}, u32[]{:S(2)}, u32[]{:S(2)}) collective-permute-start(bf16[2,2,32,4096]{3,2,1,0:T(8,128)(2,1)S(1)} %pad_maximum_fusion.14), channel_id=1, source_target_pairs={{0,2},{1,3},{2,0},{3,1},{4,6},{5,7},{6,4},{7,5},{8,10},{9,11},{10,... | collective-permute-start | bytes 3145736 | tf_op jit(solution)/shard_map/ppermute | solution.py:230
  102.8 34.1 %collective-permute-start.32 = (bf16[2,2,128,1024]{3,2,1,0:T(8,128)(2,1)S(1)}, bf16[2,2,128,1024]{3,2,1,0:T(8,128)(2,1)S(1)}, u32[]{:S(2)}, u32[]{:S(2)}) collective-permute-start(bf16[2,2,128,1024]{3,2,1,0:T(8,128)(2,1)S(1)} %pad_maximum_fusion.15), channel_id=1, source_target_pairs={{0,1},{1,0},{2,3},{3,2},{4,5},{5,4},{6,7},{7,6},{8,9},{9,8},{10,11... | collective-permute-start | bytes 3145736 | tf_op jit(solution)/shard_map/ppermute | solution.py:230
  115.3 23.8 %collective-permute-start.4 = (bf16[2,2,2,2,32,1024]{5,4,3,2,1,0:T(8,128)(2,1)S(1)}, bf16[2,2,2,2,32,1024]{5,4,3,2,1,0:T(8,128)(2,1)S(1)}, u32[]{:S(2)}, u32[]{:S(2)}) collective-permute-start(bf16[2,2,2,2,32,1024]{5,4,3,2,1,0:T(8,128)(2,1)S(1)} %pad_maximum_fusion.10), channel_id=1, source_target_pairs={{0,8},{1,9},{2,10},{3,11},{4,12},{5,13},{6,14},{7,15},{8,0},{9,1},... | collective-permute-start | bytes 3145736 | tf_op jit(solution)/shard_map/ppermute | solution.py:230
  116.4 27.9 %collective-permute-start.19 = (bf16[2,2,2,2,32,1024]{5,4,1,3,0,2:T(8,128)(2,1)}, bf16[2,2,2,2,32,1024]{5,4,1,3,0,2:T(8,128)(2,1)}, u32[]{:S(2)}, u32[]{:S(2)}) collective-permute-start(bf16[2,2,2,2,32,1024]{5,4,1,3,0,2:T(8,128)(2,1)} %pad_maximum_fusion.12), channel_id=1, source_target_pairs={{0,8},{1,9},{2,10},{3,11},{4,12},{5,13},{6,14},{7,15},{8,0},{9,1},... | collective-permute-start | bytes 3145736 | tf_op jit(solution)/shard_map/ppermute | solution.py:230
  137.0 61.4 %collective-permute-start.28 = (bf16[2,2,2,32,4096]{4,3,2,1,0:T(8,128)(2,1)}, bf16[2,2,2,32,4096]{4,3,2,1,0:T(8,128)(2,1)}, u32[]{:S(2)}, u32[]{:S(2)}) collective-permute-start(bf16[2,2,2,32,4096]{4,3,2,1,0:T(8,128)(2,1)} %pad_maximum_fusion.8), channel_id=1, source_target_pairs={{0,1},{1,0},{2,3},{3,2},{4,5},{5,4},{6,7},{7,6},{8,9},{9,8},{10,11... | collective-permute-start | bytes 6291464 | tf_op jit(solution)/shard_map/ppermute | solution.py:230
  139.0 67.9 %collective-permute-start.33 = (bf16[2,2,2,128,1024]{4,3,2,1,0:T(8,128)(2,1)}, bf16[2,2,2,128,1024]{4,3,2,1,0:T(8,128)(2,1)}, u32[]{:S(2)}, u32[]{:S(2)}) collective-permute-start(bf16[2,2,2,128,1024]{4,3,2,1,0:T(8,128)(2,1)} %pad_maximum_fusion.9), channel_id=1, source_target_pairs={{0,16},{1,17},{2,18},{3,19},{4,20},{5,21},{6,22},{7,23},{8,24},{9,... | collective-permute-start | bytes 6291464 | tf_op jit(solution)/shard_map/ppermute | solution.py:230
  156.9 55.4 %all-to-all-start = ((bf16[8,3,256,128]{3,2,1,0:T(8,128)(2,1)}), bf16[8,3,256,128]{3,2,1,0:T(8,128)(2,1)S(1)}, u32[]{:S(2)}, u32[]{:S(2)}) async-start(bf16[8,3,256,128]{3,2,1,0:T(8,128)(2,1)} %maximum_bitcast_fusion), calls=%async_computation | async-start | bytes 3145728 | tf_op jit(solution)/shard_map/all_to_all | solution.py:212
  204.1 55.4 %collective-permute-start.29 = (bf16[2,2,2,2,32,4096]{5,4,3,2,1,0:T(8,128)(2,1)}, bf16[2,2,2,2,32,4096]{5,4,3,2,1,0:T(8,128)(2,1)}, u32[]{:S(2)}, u32[]{:S(2)}) collective-permute-start(bf16[2,2,2,2,32,4096]{5,4,3,2,1,0:T(8,128)(2,1)} %pad_maximum_fusion.2), channel_id=1, source_target_pairs={{0,8},{1,9},{2,10},{3,11},{4,12},{5,13},{6,14},{7,15},{8,0},{9,1},... | collective-permute-start | bytes 12582920 | tf_op jit(solution)/shard_map/ppermute | solution.py:230
  206.5 33.2 %collective-permute-start.24 = (bf16[2,2,2,2,32,1024]{5,4,1,3,0,2:T(8,128)(2,1)}, bf16[2,2,2,2,32,1024]{5,4,1,3,0,2:T(8,128)(2,1)}, u32[]{:S(2)}, u32[]{:S(2)}) collective-permute-start(bf16[2,2,2,2,32,1024]{5,4,1,3,0,2:T(8,128)(2,1)} %pad_maximum_fusion.13), channel_id=1, source_target_pairs={{0,8},{1,9},{2,10},{3,11},{4,12},{5,13},{6,14},{7,15},{8,0},{9,1},... | collective-permute-start | bytes 3145736 | tf_op jit(solution)/shard_map/ppermute | solution.py:230
  212.2 60.3 %collective-permute-start.34 = (bf16[2,2,2,2,128,1024]{5,4,3,2,1,0:T(8,128)(2,1)}, bf16[2,2,2,2,128,1024]{5,4,3,2,1,0:T(8,128)(2,1)}, u32[]{:S(2)}, u32[]{:S(2)}) collective-permute-start(bf16[2,2,2,2,128,1024]{5,4,3,2,1,0:T(8,128)(2,1)} %pad_maximum_fusion.3), channel_id=1, source_target_pairs={{0,8},{1,9},{2,10},{3,11},{4,12},{5,13},{6,14},{7,15},{8,0},{9,1},... | collective-permute-start | bytes 12582920 | tf_op jit(solution)/shard_map/ppermute | solution.py:230
  234.5 19.9 %all-to-all-start.1 = ((bf16[8,256,128]{2,1,0:T(8,128)(2,1)}), bf16[8,256,128]{2,1,0:T(8,128)(2,1)}, u32[]{:S(2)}, u32[]{:S(2)}) async-start(bf16[8,256,128]{2,1,0:T(8,128)(2,1)} %get-tuple-element.18), calls=%async_computation.1 | async-start | bytes 1048576 | tf_op jit(solution)/shard_map/all_to_all | solution.py:212
  315.6 17.4 %collective-permute-start.55 = (bf16[2,2,2,2,32,1024]{5,4,1,3,0,2:T(8,128)(2,1)}, bf16[2,2,2,2,32,1024]{5,4,1,3,0,2:T(8,128)(2,1)}, u32[]{:S(2)}, u32[]{:S(2)}) collective-permute-start(bf16[2,2,2,2,32,1024]{5,4,1,3,0,2:T(8,128)(2,1)} %bitcast.490), channel_id=1, source_target_pairs={{0,8},{1,9},{2,10},{3,11},{4,12},{5,13},{6,14},{7,15},{8,0},{9,1},... | collective-permute-start | bytes 3145736 | tf_op jit(solution)/shard_map/ppermute | solution.py:230
  321.5 19.0 %all-to-all-start.2 = ((bf16[8,256,128]{2,1,0:T(8,128)(2,1)}), bf16[8,256,128]{2,1,0:T(8,128)(2,1)S(1)}, u32[]{:S(2)}, u32[]{:S(2)}) async-start(bf16[8,256,128]{2,1,0:T(8,128)(2,1)} %bitcast.524), calls=%async_computation.2 | async-start | bytes 1048576 | tf_op jit(solution)/shard_map/all_to_all | solution.py:212
  335.9 33.4 %collective-permute-start.56 = (bf16[2,2,2,32,1024]{4,3,1,2,0:T(8,128)(2,1)}, bf16[2,2,2,32,1024]{4,3,1,2,0:T(8,128)(2,1)}, u32[]{:S(2)}, u32[]{:S(2)}) collective-permute-start(bf16[2,2,2,32,1024]{4,3,1,2,0:T(8,128)(2,1)} %dynamic-slice_bitcast_fusion.6), channel_id=1, source_target_pairs={{0,2},{1,3},{2,0},{3,1},{4,6},{5,7},{6,4},{7,5},{8,10},{9,11},{10,... | collective-permute-start | bytes 1572872 | tf_op jit(solution)/shard_map/ppermute | solution.py:230
  365.4 44.3 %all-to-all-start.3 = ((bf16[8,3,256,128]{3,2,1,0:T(8,128)(2,1)}), bf16[8,3,256,128]{3,2,1,0:T(8,128)(2,1)S(1)}, u32[]{:S(2)}, u32[]{:S(2)}) async-start(bf16[8,3,256,128]{3,2,1,0:T(8,128)(2,1)} %attend_backward.1), calls=%async_computation.3 | async-start | bytes 3145728 | tf_op jit(solution)/shard_map/all_to_all | solution.py:212
  379.3 13.2 %collective-permute-start.58 = (bf16[2,32,1024]{2,1,0:T(8,128)(2,1)S(1)}, bf16[2,32,1024]{2,1,0:T(8,128)(2,1)S(1)}, u32[]{:S(2)}, u32[]{:S(2)}) collective-permute-start(bf16[2,32,1024]{2,1,0:T(8,128)(2,1)S(1)} %dynamic-slice_bitcast_fusion.16), channel_id=1, source_target_pairs={{0,1},{1,0},{2,3},{3,2},{4,5},{5,4},{6,7},{7,6},{8,9},{9,8},{10,11... | collective-permute-start | bytes 393224 | tf_op jit(solution)/shard_map/ppermute | solution.py:230
  392.4 46.8 %collective-permute-start.60 = (bf16[2,2,2,2,32,4096]{5,4,1,0,2,3:T(8,128)(2,1)}, bf16[2,2,2,2,32,4096]{5,4,1,0,2,3:T(8,128)(2,1)}, u32[]{:S(2)}, u32[]{:S(2)}) collective-permute-start(bf16[2,2,2,2,32,4096]{5,4,1,0,2,3:T(8,128)(2,1)} %bitcast.489), channel_id=1, source_target_pairs={{0,8},{1,9},{2,10},{3,11},{4,12},{5,13},{6,14},{7,15},{8,0},{9,1},... | collective-permute-start | bytes 12582920 | tf_op jit(solution)/shard_map/ppermute | solution.py:230
  392.5 16.5 %collective-permute-start.59 = (bf16[32,1024]{1,0:T(8,128)(2,1)S(1)}, bf16[32,1024]{1,0:T(8,128)(2,1)S(1)}, u32[]{:S(2)}, u32[]{:S(2)}) collective-permute-start(bf16[32,1024]{1,0:T(8,128)(2,1)S(1)} %dynamic-slice_bitcast_fusion.20), channel_id=1, source_target_pairs={{0,4},{1,5},{2,6},{3,7},{4,0},{5,1},{6,2},{7,3},{8,12},{9,13},{10,... | collective-permute-start | bytes 196616 | tf_op jit(solution)/shard_map/ppermute | solution.py:230
  401.1 43.6 %collective-permute-start.65 = (bf16[2,2,2,2,128,1024]{5,4,1,2,3,0:T(8,128)(2,1)}, bf16[2,2,2,2,128,1024]{5,4,1,2,3,0:T(8,128)(2,1)}, u32[]{:S(2)}, u32[]{:S(2)}) collective-permute-start(bf16[2,2,2,2,128,1024]{5,4,1,2,3,0:T(8,128)(2,1)} %bitcast.488), channel_id=1, source_target_pairs={{0,8},{1,9},{2,10},{3,11},{4,12},{5,13},{6,14},{7,15},{8,0},{9,1},... | collective-permute-start | bytes 12582920 | tf_op jit(solution)/shard_map/ppermute | solution.py:230
  428.9 21.3 %collective-permute-start.45 = (bf16[2,2,2,2,32,1024]{5,4,1,3,0,2:T(8,128)(2,1)}, bf16[2,2,2,2,32,1024]{5,4,1,3,0,2:T(8,128)(2,1)S(1)}, u32[]{:S(2)}, u32[]{:S(2)}) collective-permute-start(bf16[2,2,2,2,32,1024]{5,4,1,3,0,2:T(8,128)(2,1)} %bitcast.491), channel_id=1, source_target_pairs={{0,8},{1,9},{2,10},{3,11},{4,12},{5,13},{6,14},{7,15},{8,0},{9,1},... | collective-permute-start | bytes 3145736 | tf_op jit(solution)/shard_map/ppermute | solution.py:230
  431.1 19.6 %collective-permute-start.35 = (bf16[2,2,2,2,32,1024]{5,4,1,2,3,0:T(8,128)(2,1)}, bf16[2,2,2,2,32,1024]{5,4,1,2,3,0:T(8,128)(2,1)S(1)}, u32[]{:S(2)}, u32[]{:S(2)}) collective-permute-start(bf16[2,2,2,2,32,1024]{5,4,1,2,3,0:T(8,128)(2,1)} %bitcast.493), channel_id=1, source_target_pairs={{0,8},{1,9},{2,10},{3,11},{4,12},{5,13},{6,14},{7,15},{8,0},{9,1},... | collective-permute-start | bytes 3145736 | tf_op jit(solution)/shard_map/ppermute | solution.py:230
  438.0 14.8 %collective-permute-start.40 = (bf16[2,2,2,2,32,1024]{5,4,1,0,2,3:T(8,128)(2,1)}, bf16[2,2,2,2,32,1024]{5,4,1,0,2,3:T(8,128)(2,1)}, u32[]{:S(2)}, u32[]{:S(2)}) collective-permute-start(bf16[2,2,2,2,32,1024]{5,4,1,0,2,3:T(8,128)(2,1)} %bitcast.492), channel_id=1, source_target_pairs={{0,8},{1,9},{2,10},{3,11},{4,12},{5,13},{6,14},{7,15},{8,0},{9,1},... | collective-permute-start | bytes 3145736 | tf_op jit(solution)/shard_map/ppermute | solution.py:230
  443.2 82.4 %collective-permute-start.61 = (bf16[2,2,2,32,4096]{4,3,1,0,2:T(8,128)(2,1)S(1)}, bf16[2,2,2,32,4096]{4,3,1,0,2:T(8,128)(2,1)S(1)}, u32[]{:S(2)}, u32[]{:S(2)}) collective-permute-start(bf16[2,2,2,32,4096]{4,3,1,0,2:T(8,128)(2,1)S(1)} %dynamic-slice_bitcast_fusion.1), channel_id=1, source_target_pairs={{0,1},{1,0},{2,3},{3,2},{4,5},{5,4},{6,7},{7,6},{8,9},{9,8},{10,11... | collective-permute-start | bytes 6291464 | tf_op jit(solution)/shard_map/ppermute | solution.py:230
  449.6 81.3 %collective-permute-start.66 = (bf16[2,2,2,128,1024]{4,3,0,1,2:T(8,128)(2,1)S(1)}, bf16[2,2,2,128,1024]{4,3,0,1,2:T(8,128)(2,1)S(1)}, u32[]{:S(2)}, u32[]{:S(2)}) collective-permute-start(bf16[2,2,2,128,1024]{4,3,0,1,2:T(8,128)(2,1)S(1)} %dynamic-slice_bitcast_fusion), channel_id=1, source_target_pairs={{0,16},{1,17},{2,18},{3,19},{4,20},{5,21},{6,22},{7,23},{8,24},{9,... | collective-permute-start | bytes 6291464 | tf_op jit(solution)/shard_map/ppermute | solution.py:230
  450.7 14.1 %collective-permute-start.46 = (bf16[2,2,2,32,1024]{4,3,1,2,0:T(8,128)(2,1)S(1)}, bf16[2,2,2,32,1024]{4,3,1,2,0:T(8,128)(2,1)S(1)}, u32[]{:S(2)}, u32[]{:S(2)}) collective-permute-start(bf16[2,2,2,32,1024]{4,3,1,2,0:T(8,128)(2,1)S(1)} %dynamic-slice_bitcast_fusion.7), channel_id=1, source_target_pairs={{0,2},{1,3},{2,0},{3,1},{4,6},{5,7},{6,4},{7,5},{8,10},{9,11},{10,... | collective-permute-start | bytes 1572872 | tf_op jit(solution)/shard_map/ppermute | solution.py:230
  451.3 58.1 %collective-permute-start.36 = (bf16[2,2,2,32,1024]{4,3,0,1,2:T(8,128)(2,1)S(1)}, bf16[2,2,2,32,1024]{4,3,0,1,2:T(8,128)(2,1)S(1)}, u32[]{:S(2)}, u32[]{:S(2)}) collective-permute-start(bf16[2,2,2,32,1024]{4,3,0,1,2:T(8,128)(2,1)S(1)} %dynamic-slice_bitcast_fusion.9), channel_id=1, source_target_pairs={{0,16},{1,17},{2,18},{3,19},{4,20},{5,21},{6,22},{7,23},{8,24},{9,... | collective-permute-start | bytes 1572872 | tf_op jit(solution)/shard_map/ppermute | solution.py:230
  454.5 56.6 %collective-permute-start.41 = (bf16[2,2,2,32,1024]{4,3,1,0,2:T(8,128)(2,1)S(1)}, bf16[2,2,2,32,1024]{4,3,1,0,2:T(8,128)(2,1)S(1)}, u32[]{:S(2)}, u32[]{:S(2)}) collective-permute-start(bf16[2,2,2,32,1024]{4,3,1,0,2:T(8,128)(2,1)S(1)} %dynamic-slice_bitcast_fusion.8), channel_id=1, source_target_pairs={{0,1},{1,0},{2,3},{3,2},{4,5},{5,4},{6,7},{7,6},{8,9},{9,8},{10,11... | collective-permute-start | bytes 1572872 | tf_op jit(solution)/shard_map/ppermute | solution.py:230
  465.1 49.5 %collective-permute-start.47 = (bf16[2,2,32,1024]{3,2,0,1:T(8,128)(2,1)S(1)}, bf16[2,2,32,1024]{3,2,0,1:T(8,128)(2,1)S(1)}, u32[]{:S(2)}, u32[]{:S(2)}) collective-permute-start(bf16[2,2,32,1024]{3,2,0,1:T(8,128)(2,1)S(1)} %dynamic-slice_bitcast_fusion.13), channel_id=1, source_target_pairs={{0,16},{1,17},{2,18},{3,19},{4,20},{5,21},{6,22},{7,23},{8,24},{9,... | collective-permute-start | bytes 786440 | tf_op jit(solution)/shard_map/ppermute | solution.py:230
  526.7 25.3 %collective-permute-start.62 = (bf16[2,2,32,4096]{3,2,1,0:T(8,128)(2,1)S(1)}, bf16[2,2,32,4096]{3,2,1,0:T(8,128)(2,1)S(1)}, u32[]{:S(2)}, u32[]{:S(2)}) collective-permute-start(bf16[2,2,32,4096]{3,2,1,0:T(8,128)(2,1)S(1)} %dynamic-slice_bitcast_fusion.3), channel_id=1, source_target_pairs={{0,2},{1,3},{2,0},{3,1},{4,6},{5,7},{6,4},{7,5},{8,10},{9,11},{10,... | collective-permute-start | bytes 3145736 | tf_op jit(solution)/shard_map/ppermute | solution.py:230
  532.0 23.3 %collective-permute-start.67 = (bf16[2,2,128,1024]{3,2,0,1:T(8,128)(2,1)S(1)}, bf16[2,2,128,1024]{3,2,0,1:T(8,128)(2,1)S(1)}, u32[]{:S(2)}, u32[]{:S(2)}) collective-permute-start(bf16[2,2,128,1024]{3,2,0,1:T(8,128)(2,1)S(1)} %dynamic-slice_bitcast_fusion.2), channel_id=1, source_target_pairs={{0,1},{1,0},{2,3},{3,2},{4,5},{5,4},{6,7},{7,6},{8,9},{9,8},{10,11... | collective-permute-start | bytes 3145736 | tf_op jit(solution)/shard_map/ppermute | solution.py:230
  552.2 12.8 %collective-permute-start.63 = (bf16[2,32,4096]{2,1,0:T(8,128)(2,1)S(1)}, bf16[2,32,4096]{2,1,0:T(8,128)(2,1)S(1)}, u32[]{:S(2)}, u32[]{:S(2)}) collective-permute-start(bf16[2,32,4096]{2,1,0:T(8,128)(2,1)S(1)} %dynamic-slice_bitcast_fusion.5), channel_id=1, source_target_pairs={{0,16},{1,17},{2,18},{3,19},{4,20},{5,21},{6,22},{7,23},{8,24},{9,... | collective-permute-start | bytes 1572872 | tf_op jit(solution)/shard_map/ppermute | solution.py:230
  555.8 11.3 %collective-permute-start.68 = (bf16[2,128,1024]{2,1,0:T(8,128)(2,1)S(1)}, bf16[2,128,1024]{2,1,0:T(8,128)(2,1)S(1)}, u32[]{:S(2)}, u32[]{:S(2)}) collective-permute-start(bf16[2,128,1024]{2,1,0:T(8,128)(2,1)S(1)} %dynamic-slice_bitcast_fusion.4), channel_id=1, source_target_pairs={{0,2},{1,3},{2,0},{3,1},{4,6},{5,7},{6,4},{7,5},{8,10},{9,11},{10,... | collective-permute-start | bytes 1572872 | tf_op jit(solution)/shard_map/ppermute | solution.py:230
  565.2 18.7 %collective-permute-start.64 = (bf16[32,4096]{1,0:T(8,128)(2,1)S(1)}, bf16[32,4096]{1,0:T(8,128)(2,1)S(1)}, u32[]{:S(2)}, u32[]{:S(2)}) collective-permute-start(bf16[32,4096]{1,0:T(8,128)(2,1)S(1)} %dynamic-slice_bitcast_fusion.11), channel_id=1, source_target_pairs={{0,4},{1,5},{2,6},{3,7},{4,0},{5,1},{6,2},{7,3},{8,12},{9,13},{10,... | collective-permute-start | bytes 786440 | tf_op jit(solution)/shard_map/ppermute | solution.py:230
  567.4 21.4 %collective-permute-start.69 = (bf16[128,1024]{1,0:T(8,128)(2,1)S(1)}, bf16[128,1024]{1,0:T(8,128)(2,1)S(1)}, u32[]{:S(2)}, u32[]{:S(2)}) collective-permute-start(bf16[128,1024]{1,0:T(8,128)(2,1)S(1)} %dynamic-slice_bitcast_fusion.10), channel_id=1, source_target_pairs={{0,4},{1,5},{2,6},{3,7},{4,0},{5,1},{6,2},{7,3},{8,12},{9,13},{10,... | collective-permute-start | bytes 786440 | tf_op jit(solution)/shard_map/ppermute | solution.py:230
  (78 other events, 516.0 us)
